TPU v7x, 256 devices: a whole 4x4x8 slice. The times are simulated.
256 devices in a mesh: row: 8 (over y_hi, x), col: 32 (over z, y_lo, core).
Axes of the slice: x: 4, y: 4 (y_hi: 2, y_lo: 2; y = y_hi * 2 + y_lo), z: 8, core: 2. Of those that a mesh axis runs over, the one named last changes fastest.
Arguments:
- inputs: bfloat16 [1024, 12288], P('col', 'row'), may hold values from -6 to 6
- grad_out: bfloat16 [1024, 12288], P('col', 'row'), may hold values from -6 to 6
- pre_act: bfloat16 [1024, 24576], P('row', 'col'), may hold values from -6 to 6
- w_in: bfloat16 [12288, 24576], P('row', 'col'), may hold values from -0.0390625 to 0.0390625
- w_out: bfloat16 [24576, 12288], P('col', 'row'), may hold values from -0.0546875 to 0.0546875
- mask_in: int32 [96, 192], P('row', 'col'), may hold values from 0 to 1, as said below
- mask_out: int32 [192, 96], P('col', 'row'), may hold values from 0 to 1, as said below
Outputs:
- grad_inputs: bfloat16 [1024, 12288], P('col', 'row')
- grad_w_in: bfloat16 [12288, 24576], P('row', 'col')
- grad_w_out: bfloat16 [24576, 12288], P('col', 'row')
Inputs may be any that keep to these rules, and one draw needn't show every extreme that they name: `mask_in`: each entry is 0 or 1; the share of ones differs from one row of tiles to another. `mask_out`: each entry is 0 or 1; the share of ones differs from one row of tiles to another.
All inputs are finite; a program needn't handle non-finite values.
Results may differ from a plain program's by a relative error of at most 0.0049.
Values may be sent and summed in bfloat16 or wider, within the bound.
No kernel may reach another device: no remote copies, remote signals or barrier semaphores. Data moves between devices by JAX's collectives and lax.ppermute only.
A program may use at most 128 MiB of HBM per device.

v0:
```python
import functools
import math

import jax
import jax.numpy as jnp
from jax import lax
from jax.experimental import pallas as pl
from jax.experimental.pallas import tpu as pltpu
from jax.sharding import Mesh
from jax.sharding import PartitionSpec as P

coef = math.sqrt(2.0 / math.pi)
VMEM = 16
BF = jnp.bfloat16
F32 = jnp.float32
SIZE = {"yhi": 2, "x": 4, "z": 8, "ylo": 2, "core": 2}
TO_X = (
    (2, 1, BF),
    (-1, 1, BF),
    (1, 1, F32),
    (2, 0, BF),
    (1, 0, BF),
    (-1, 0, F32),
    (0, 0, F32),
    (0, 1, F32),
)
FROM_X = ((0, 0), (0, 1), (-1, 0), (1, 0), (-1, 1), (1, 1), (2, 0), (2, 1))
NT = (((1,), (1,)), ((), ()))
TN = (((0,), (0,)), ((), ()))
MIB = 1 << 20


def shift(value, axis, by):
    count = SIZE[axis]
    return lax.ppermute(value, axis, [(i, (i + by) % count) for i in range(count)])


def params(mib):
    return pltpu.CompilerParams(vmem_limit_bytes=mib * MIB)


def cost(flops, size):
    return pl.CostEstimate(flops=flops, bytes_accessed=size, transcendentals=0)


def after(value, *others):
    return lax.optimization_barrier((value, *others))[0]


def together(*values):
    return lax.optimization_barrier(values)


def both_ways(axis, up, down):
    return shift(up, axis, 1), shift(down, axis, -1)


def plan_z(count):
    half = lambda off, kind, at: [(at, off, 0, kind), (at + count, off, 1, kind)]
    both = lambda off: half(off, 0, 0) + half(off, 1, 2 * count)
    plan = [both(0)]
    for step in range(1, 4):
        plan += [both(-step), both(step)]
    return plan + [half(4, 0, 0), half(4, 1, 0)]


def plan_x(count):
    both = lambda off: [(0, off, 0), (count, off, 1)]
    return [both(0), both(-1), both(1), both(2)]


def whole(shape):
    return pl.BlockSpec(shape, lambda *_: (0,) * len(shape))


def place_z(pos, off, half, count):
    owner = lax.rem(pos[2] + (off + 8), 8)
    return pl.multiple_of(owner * (2 * count) + lax.rem(pos[3] + half, 2) * count, 16)


def place_x(pos, off, half, count):
    owner = lax.rem(pos[0] + half, 2) * 4 + lax.rem(pos[1] + (off + 4), 4)
    return pl.multiple_of(owner * count, 16)


def in_vmem(count):
    return [pl.BlockSpec(memory_space=pltpu.VMEM)] * count


def call(kernel, name, pos, arrays, shapes, scratch, flops):
    return pl.pallas_call(
        kernel,
        in_specs=[pl.BlockSpec(memory_space=pltpu.SMEM)] + in_vmem(len(arrays)),
        out_specs=in_vmem(len(shapes)),
        out_shape=[jax.ShapeDtypeStruct(n, t) for n, t in shapes],
        scratch_shapes=scratch,
        compiler_params=params(VMEM),
        cost_estimate=cost(flops, MIB),
        name=name,
    )(pos, *arrays)


def kept(mask, row, col, values):
    return jnp.where(mask[row, col] > 0, values, jnp.zeros_like(values))


def mask_kernel(mask_out, mask_in, w_out, w_in, theirs, out):
    out[1536:1600, 0:768] = theirs[...]
    out[1536:1600, 768:1536] = theirs[...]

    @pl.loop(0, 6)
    def _(i):
        rows = pl.ds(pl.multiple_of(i * 128, 128), 128)
        later = pl.ds(pl.multiple_of(i * 128 + 768, 128), 128)
        for j in range(12):
            cols = slice(j * 128, j * 128 + 128)
            out[rows, cols] = kept(mask_out, i, j, w_out[rows, cols])
            side, tile = j // 6, j % 6
            source = pl.ds(pl.multiple_of(i * 128 + side * 768, 128), 128)
            part = w_in[source, tile * 128 : tile * 128 + 128]
            out[later, cols] = kept(mask_in, i + side * 6, tile, part)


def masked(mask_out, mask_in, w_out, w_in, theirs):
    return pl.pallas_call(
        mask_kernel,
        in_specs=[pl.BlockSpec(memory_space=pltpu.SMEM)] * 2 + in_vmem(3),
        out_specs=pl.BlockSpec(memory_space=pltpu.VMEM),
        out_shape=jax.ShapeDtypeStruct((1600, 1536), BF),
        compiler_params=params(VMEM),
        cost_estimate=cost(0, 4 * MIB),
        name="masked",
    )(mask_out, mask_in, w_out, w_in, theirs)


def values_kernel(pos, pre, hidden, slopes, other):
    core = pos[4]
    zval = pre[...].astype(F32)
    tval = jnp.tanh(coef * (zval + 0.044715 * zval**3))
    hidden[...] = (0.5 * zval * (1.0 + tval)).astype(BF)
    for half in range(2):
        mine = pl.ds(pl.multiple_of(half * 64 + core * 32, 32), 32)
        theirs = pl.ds(pl.multiple_of(half * 64 + (1 - core) * 32, 32), 32)
        rows = slice(half * 32, half * 32 + 32)
        slopes[rows, :] = slope(pre[mine, :])
        other[rows, :] = pre[theirs, :]


def first_kernel(plan, count, pos, *refs):
    pieces = refs[: len(plan)]
    own_ref, peer_ref, rows = refs[len(plan) : len(plan) + 3]
    outs, held = refs[len(plan) + 3 : -1], refs[-1]
    two = 2 * count
    for ref, spots in zip(pieces, plan):
        for first, off, half, kind in spots:
            at = pl.ds(place_z(pos, off, half, count) + kind * 16 * count, count)
            rows[at, :] = ref[first : first + count, :]

    for half, weight in enumerate((own_ref, peer_ref)):
        held[...] = lax.dot_general(
            rows[0 : 16 * count, :], weight[0:768, :], NT, preferred_element_type=F32
        )
        where = slice(half * 768, half * 768 + 768)

        for ref, (off, y, _) in zip(outs, TO_X):
            block = held[pl.ds(place_x(pos, off, y, two), two), :]
            ref[:, where] = block.astype(ref.dtype)


def first(pos, pieces, own, peer, count):
    tokens, two = 16 * count, 2 * count
    heights = [(2 * tokens, BF)] + [(two, kind) for _, _, kind in TO_X]
    return call(
        functools.partial(first_kernel, plan_z(count), count),
        "first",
        pos,
        [*pieces, own, peer],
        [((n, 1536), t) for n, t in heights],
        [pltpu.VMEM((tokens, 768), F32)],
        4 * tokens * 1536 * 1536,
    )


def second_kernel(count, pos, *refs):
    pieces, refs = refs[: len(FROM_X)], refs[len(FROM_X) :]
    own_ref, peer_ref, rows, rows_peer = refs[:4]
    outs = refs[4:-1]
    held = refs[-1]
    two = 2 * count
    wide = held.shape[1]
    for ref, (off, y) in zip(pieces, FROM_X):
        at = pl.ds(place_x(pos, off, y, two), two)
        rows[at, :] = ref[:, 0:768]
        rows_peer[at, :] = ref[:, 768:1536]

    for step in range(1536 // wide):
        where = slice(step * wide, step * wide + wide)
        out = lax.dot_general(rows[...], own_ref[768:1536, where], NT, preferred_element_type=F32)
        out += lax.dot_general(rows_peer[...], peer_ref[768:1536, where], NT, preferred_element_type=F32)
        held[...] = out

        def block(off, half):
            return held[pl.ds(place_z(pos, off, half, count), count), :]

        up, down, keep = outs[0:4], outs[4:8], outs[8]
        for s in range(4):
            kind = BF if s == 0 else F32
            up[s][0:count, where] = block(4 - s, 0).astype(kind)
            down[s][0:count, where] = block(s - 4, 1).astype(kind)
            if s < 3:
                up[s][count:two, where] = block(3 - s, 1).astype(kind)
                down[s][count:two, where] = block(s - 3, 0).astype(kind)
        keep[0:count, where] = block(0, 0)
        keep[count:two, where] = block(0, 1)


def second(pos, pieces, own, peer, count):
    tokens, two = 16 * count, 2 * count
    ring = [(two, BF), (two, F32), (two, F32), (count, F32)]
    shapes = [((tokens, 768), BF)] * 2
    shapes += [((n, 1536), t) for n, t in ring + ring + [(two, F32)]]
    return call(
        functools.partial(second_kernel, count),
        "second",
        pos,
        [*pieces, own, peer],
        shapes,
        [pltpu.VMEM((tokens, 768), F32)],
        4 * tokens * 1536 * 1536,
    )


def store_kept(total, mask, first, out):
    for i in range(out.shape[0] // 128):
        rows = slice(i * 128, i * 128 + 128)
        for j in range(out.shape[1] // 128):
            cols = slice(j * 128, j * 128 + 128)
            out[rows, cols] = kept(mask, first + i, j, total[rows, cols]).astype(BF)


def wout_kernel(plan, pos, mask, *refs):
    pieces = refs[: len(plan)]
    own, peer, out, held = refs[len(plan) :]
    for ref, spots in zip(pieces, plan):
        for first, off, half in spots:
            owner = lax.rem(pos[0] + half, 2) * 4 + lax.rem(pos[1] + (off + 4), 4)
            held[owner] = ref[first : first + 128, :].reshape(2, 2, 32, -1)
    total = None
    for k, part in enumerate((own, peer)):
        left = held[:, :, lax.rem(pos[4] + k, 2)].reshape(512, -1)
        term = lax.dot_general(left, part[0:512, :], TN, preferred_element_type=F32)
        total = term if total is None else total + term
    store_kept(total, mask, pl.program_id(0) * (out.shape[0] // 128), out)


def wout_grad(pos, pieces, own, peer, mask):
    block = 384
    return pl.pallas_call(
        functools.partial(wout_kernel, plan_x(128)),
        grid_spec=pltpu.PrefetchScalarGridSpec(
            num_scalar_prefetch=2,
            grid=(768 // block,),
            in_specs=[pl.BlockSpec((a.shape[0], block), lambda i, *_: (0, i)) for a in pieces]
            + in_vmem(2),
            out_specs=pl.BlockSpec((block, 1536), lambda i, *_: (i, 0)),
            scratch_shapes=[pltpu.VMEM((8, 2, 2, 32, block), BF)],
        ),
        out_shape=jax.ShapeDtypeStruct((768, 1536), BF),
        compiler_params=params(VMEM),
        cost_estimate=cost(4 * 1024 * 1536 * 768, 8 * MIB),
        name="wout_grad",
    )(pos, mask, *pieces, own, peer)


def win_kernel(mask, left0, left1, own, peer, out):
    total = None
    for left, right in ((left0, own), (left1, peer)):
        term = lax.dot_general(left[...], right[...], TN, preferred_element_type=F32)
        total = term if total is None else total + term
    store_kept(total, mask, pl.program_id(0) * (out.shape[0] // 128), out)


def win_grad(own_rows, peer_rows, own, peer, mask):
    block = 768
    rows = pl.BlockSpec((512, block), lambda i, _: (1, i))
    return pl.pallas_call(
        win_kernel,
        grid_spec=pltpu.PrefetchScalarGridSpec(
            num_scalar_prefetch=1,
            grid=(1536 // block,),
            in_specs=[rows, rows] + in_vmem(2),
            out_specs=pl.BlockSpec((block, 768), lambda i, _: (i, 0)),
        ),
        out_shape=jax.ShapeDtypeStruct((1536, 768), BF),
        compiler_params=params(VMEM),
        cost_estimate=cost(4 * 1024 * 1536 * 768, 8 * MIB),
        name="win_grad",
    )(mask, own_rows, peer_rows, own, peer)


def slope(values):
    zval = values.astype(F32)
    tval = jnp.tanh(coef * (zval + 0.044715 * zval**3))
    return 0.5 * (1.0 + tval) + 0.5 * zval * (1.0 - tval * tval) * coef * (
        1.0 + 3.0 * 0.044715 * zval * zval
    )


def body(inputs, grad_out, pre_act, w_in, w_out, mask_in, mask_out):
    names = ("yhi", "x", "z", "ylo", "core")
    pos = jnp.stack([lax.axis_index(n) for n in names]).astype(jnp.int32)
    f = lambda v: v.astype(F32)
    count, two = 32, 64

    others = [shift(v, "ylo", 1) for v in (grad_out, inputs)]
    shapes = [((128, 768), BF), ((64, 768), F32), ((64, 768), BF)]
    hidden, slopes, theirs = call(values_kernel, "values", pos, [pre_act], shapes, [], MIB)
    hidden_other = shift(hidden, "yhi", 1)
    *others, hidden, theirs = together(*others, hidden, theirs)
    sent = jnp.concatenate([grad_out, others[0], inputs, others[1]])
    up1, down1 = both_ways("z", sent, sent)
    own = masked(after(mask_out, sent), mask_in, w_out, w_in, theirs)
    up1, down1, own, hidden_other = together(up1, down1, own, hidden_other)
    up2, down2 = both_ways("z", up1, down1)
    peer = shift(own, "core", 1)
    hid = jnp.concatenate([hidden, hidden_other])
    hid_up, hid_down = both_ways("x", hid, hid)
    up2, down2 = together(up2, down2)
    up3, down3 = both_ways("z", up2, down2)
    up3, down3, hid_up, hid_down = together(up3, down3, hid_up, hid_down)
    up4, down4 = both_ways("z", up3[: 2 * count], down3[2 * count :])
    hid_far = shift(after(hid_up, up3), "x", 1)
    up4, down4, hid_far = together(up4, down4, hid_far)
    pieces = [sent, up1, down1, up2, down2, up3, down3, up4, down4]

    rows, far1, down1, up1, far0, up0, down0, keep0, keep1 = first(pos, pieces, own, peer, count)
    got, down1 = both_ways("x", far1, down1)
    slopes = jnp.concatenate([slopes, slope(after(peer, keep1)[1536:, :768])], axis=1)
    rows_peer = shift(after(rows, slopes), "core", 1)
    got, down1, slopes = together(got, down1, slopes)
    up1, got = both_ways("x", (up1 + f(got)).astype(BF), far0)
    up1, got = together(up1, got)
    other = shift((keep1 + f(down1) + f(up1)).astype(BF), "yhi", 1)
    up0, down0 = both_ways("x", up0, (down0 + f(got)).astype(BF))
    act = ((keep0 + f(up0) + f(down0) + f(other)) * slopes).astype(BF)

    other = shift(act, "yhi", 1)
    up0, down0 = both_ways("x", act, act)
    hidden_pieces = [hid, hid_up, hid_down, hid_far]
    grad_w_out = wout_grad(pos, hidden_pieces, rows, after(rows_peer, act), mask_out)
    other, up0, down0, grad_w_out = together(other, up0, down0, grad_w_out)
    up1, down1 = both_ways("x", other, other)
    far0 = shift(up0, "x", 1)
    far1 = shift(down1, "x", -1)

    acts = [act, other, up0, down0, up1, down1, far0, far1]
    outs = second(pos, acts, own, peer, count)
    acts_own, acts_peer = outs[0:2]
    up, down, keep = outs[2:6], outs[6:10], outs[10]
    send_up, send_down = up[0], down[0]
    for s in range(1, 4):
        got_up, got_down = shift(send_up, "z", 1), shift(send_down, "z", -1)
        if s == 1:
            acts_peer = shift(acts_peer, "core", 1)
        elif s == 2:
            grad_w_in = win_grad(
                rows, rows_peer, acts_own, after(acts_peer, send_up, send_down), mask_in
            )
            got_up, got_down, _ = lax.optimization_barrier((got_up, got_down, grad_w_in))
        n = two if s < 3 else count
        send_up = (up[s] + f(got_up[:n])).astype(BF)
        send_down = (down[s] + f(got_down[:n])).astype(BF)
    end_up, end_down = shift(send_up, "z", 1), shift(send_down, "z", -1)
    send = (keep[count:] + f(got_up[count:]) + f(end_down)).astype(BF)
    mine = keep[:count] + f(got_down[count:]) + f(end_up)
    grad_inputs = (mine + f(shift(send, "ylo", 1))).astype(BF)
    return grad_inputs, grad_w_in, grad_w_out


def solution(mesh):
    fine = Mesh(mesh.devices.reshape(2, 4, 8, 2, 2), ("yhi", "x", "z", "ylo", "core"))
    row, col = ("yhi", "x"), ("z", "ylo", "core")
    return jax.shard_map(
        body,
        mesh=fine,
        in_specs=(
            P(col, row),
            P(col, row),
            P(row, col),
            P(row, col),
            P(col, row),
            P(row, col),
            P(col, row),
        ),
        out_specs=(P(col, row), P(row, col), P(col, row)),
        check_vma=False,
    )
```

profile of v0, /device:TPU:6, one launch (start us, length us, event | category | flops | bytes accessed | tf_op | source)
XLA Modules:
  0.0 154.4 jit_solution(17249275065313582380)
XLA Ops:
  0.6 1.7 %collective-permute-start.1 = (bf16[32,1536]{1,0:T(8,128)(2,1)}, bf16[32,1536]{1,0:T(8,128)(2,1)S(1)}, u32[]{:S(2)}, u32[]{:S(2)}) collective-permute-start(bf16[32,1536]{1,0:T(8,128)(2,1)} %param.7), channel_id=1, source_target_pairs={{0,2},{2,0},{1,3},{3,1},{4,6},{6,4},{5,7},{7,5},{8,10},{10,8},{9,1... | collective-permute-start | bytes 294920 | tf_op jit(solution)/shard_map/ppermute | solution.py:35
  2.3 0.4 collective-permute-start
  2.7 0.9 constant_dynamic-update-slice_fusion.3
  3.7 0.1 stack.23.pos
  3.8 0.9 copy-done.2
  4.7 0.8 values.1
  5.5 0.9 collective-permute-done.1
  6.4 1.2 collective-permute-done
  7.7 0.9 constant_dynamic-update-slice_fusion.1
  8.6 5.9 %collective-permute-start.3 = (bf16[128,1536]{1,0:T(8,128)(2,1)S(1)}, bf16[128,1536]{1,0:T(8,128)(2,1)S(1)}, u32[]{:S(2)}, u32[]{:S(2)}) collective-permute-start(bf16[128,1536]{1,0:T(8,128)(2,1)S(1)} %constant_dynamic-update-slice_fusion.refs_0_), channel_id=1, source_target_pairs={{0,28},{4,0},{8,4},{12,8},{16,12},{20,16},{24,20},{28,24},{1,29},{... | collective-permute-start | bytes 1179656 | tf_op jit(solution)/shard_map/ppermute | solution.py:35
  14.5 3.1 %collective-permute-start.4 = (bf16[128,768]{1,0:T(8,128)(2,1)S(1)}, bf16[128,768]{1,0:T(8,128)(2,1)S(1)}, u32[]{:S(2)}, u32[]{:S(2)}) collective-permute-start(bf16[128,768]{1,0:T(8,128)(2,1)S(1)} %get-tuple-element.70), channel_id=1, source_target_pairs={{0,128},{128,0},{1,129},{129,1},{2,130},{130,2},{3,131},{131,3},{4... | collective-permute-start | bytes 589832 | tf_op jit(solution)/shard_map/ppermute | solution.py:35
  17.6 0.8 copy.10.mask_in.mask
  18.4 1.7 %copy-done = bf16[768,1536]{1,0:T(8,128)(2,1)S(1)} copy-done((bf16[768,1536]{1,0:T(8,128)(2,1)S(1)}, bf16[768,1536]{1,0:T(8,128)(2,1)}, u32[]{:S(2)}) %copy-start) | copy-done | bytes 2359320
  20.1 1.7 %copy-done.1 = bf16[1536,768]{1,0:T(8,128)(2,1)S(1)} copy-done((bf16[1536,768]{1,0:T(8,128)(2,1)S(1)}, bf16[1536,768]{1,0:T(8,128)(2,1)}, u32[]{:S(2)}) %copy-start.1) | copy-done | bytes 2359320
  21.7 0.7 copy-done.3
  22.4 2.1 %masked.1.refs_9_.refs_8_ = bf16[1600,1536]{1,0:T(8,128)(2,1)S(1)} custom-call(s32[6,12]{1,0:T(8,128)S(1)} %copy-done.3, s32[12,6]{1,0:T(8,128)S(1)} %copy.10.mask_in.mask, bf16[768,1536]{1,0:T(8,128)(2,1)S(1)} %copy-done, bf16[1536,768]{1,0:T(8,128)(2,1)S(1)} %copy-done.1, bf16[64,768]{1,0:T(8,128)(2,1)S(1)} %get-tuple-element.65.theirs), custom_call_target="tpu_custom_call" | custom-call | bytes 4194304 | tf_op jit(solution)/shard_map/masked/pallas_call | solution.py:125
  24.6 1.1 collective-permute-done.2.refs_1_
  25.7 3.2 %collective-permute-start.6 = (bf16[128,1536]{1,0:T(8,128)(2,1)S(1)}, bf16[128,1536]{1,0:T(8,128)(2,1)S(1)}, u32[]{:S(2)}, u32[]{:S(2)}) collective-permute-start(bf16[128,1536]{1,0:T(8,128)(2,1)S(1)} %collective-permute-done.3.refs_2_), channel_id=1, source_target_pairs={{0,28},{4,0},{8,4},{12,8},{16,12},{20,16},{24,20},{28,24},{1,29},{... | collective-permute-start | bytes 1179656 | tf_op jit(solution)/shard_map/ppermute | solution.py:35
  29.0 0.9 collective-permute-start.10
  29.9 2.4 %collective-permute-start.9 = (bf16[256,768]{1,0:T(8,128)(2,1)S(1)}, bf16[256,768]{1,0:T(8,128)(2,1)S(1)}, u32[]{:S(2)}, u32[]{:S(2)}) collective-permute-start(bf16[256,768]{1,0:T(8,128)(2,1)S(1)} %constant_dynamic-update-slice_fusion.4.refs_0_), channel_id=1, source_target_pairs={{0,32},{32,64},{64,96},{96,0},{1,33},{33,65},{65,97},{97,1},{2,34}... | collective-permute-start | bytes 1179656 | tf_op jit(solution)/shard_map/ppermute | solution.py:35
  32.3 6.1 %collective-permute-done.5.refs_3_ = bf16[128,1536]{1,0:T(8,128)(2,1)S(1)} collective-permute-done((bf16[128,1536]{1,0:T(8,128)(2,1)S(1)}, bf16[128,1536]{1,0:T(8,128)(2,1)S(1)}, u32[]{:S(2)}, u32[]{:S(2)}) %collective-permute-start.5) | collective-permute-done | bytes 393248 | tf_op jit(solution)/shard_map/ppermute | solution.py:35
  38.4 3.2 %collective-permute-start.8 = (bf16[128,1536]{1,0:T(8,128)(2,1)S(1)}, bf16[128,1536]{1,0:T(8,128)(2,1)S(1)}, u32[]{:S(2)}, u32[]{:S(2)}) collective-permute-start(bf16[128,1536]{1,0:T(8,128)(2,1)S(1)} %collective-permute-done.6.refs_4_), channel_id=1, source_target_pairs={{0,28},{4,0},{8,4},{12,8},{16,12},{20,16},{24,20},{28,24},{1,29},{... | collective-permute-start | bytes 1179656 | tf_op jit(solution)/shard_map/ppermute | solution.py:35
  41.7 8.7 %collective-permute-done.7.refs_5_ = bf16[128,1536]{1,0:T(8,128)(2,1)S(1)} collective-permute-done((bf16[128,1536]{1,0:T(8,128)(2,1)S(1)}, bf16[128,1536]{1,0:T(8,128)(2,1)S(1)}, u32[]{:S(2)}, u32[]{:S(2)}) %collective-permute-start.7) | collective-permute-done | bytes 393248 | tf_op jit(solution)/shard_map/ppermute | solution.py:35
  50.4 0.5 collective-permute-start.13
  50.9 0.2 collective-permute-start.11
  51.1 3.1 %collective-permute-start.12 = (bf16[64,1536]{1,0:T(8,128)(2,1)S(1)}, bf16[64,1536]{1,0:T(8,128)(2,1)S(1)}, u32[]{:S(2)}, u32[]{:S(2)}) collective-permute-start(bf16[64,1536]{1,0:T(8,128)(2,1)S(1)} %slice.28), channel_id=1, source_target_pairs={{0,28},{4,0},{8,4},{12,8},{16,12},{20,16},{24,20},{28,24},{1,29},{... | collective-permute-start | bytes 589832 | tf_op jit(solution)/shard_map/ppermute | solution.py:35
  54.2 3.6 %collective-permute-done.11.refs_7_ = bf16[64,1536]{1,0:T(8,128)(2,1)S(1)} collective-permute-done((bf16[64,1536]{1,0:T(8,128)(2,1)S(1)}, bf16[64,1536]{1,0:T(8,128)(2,1)S(1)}, u32[]{:S(2)}, u32[]{:S(2)}) %collective-permute-start.11) | collective-permute-done | bytes 196640 | tf_op jit(solution)/shard_map/ppermute | solution.py:35
  57.9 2.4 %collective-permute-done.13.refs_3_ = bf16[256,768]{1,0:T(8,128)(2,1)S(1)} collective-permute-done((bf16[256,768]{1,0:T(8,128)(2,1)S(1)}, bf16[256,768]{1,0:T(8,128)(2,1)S(1)}, u32[]{:S(2)}, u32[]{:S(2)}) %collective-permute-start.13) | collective-permute-done | bytes 393248 | tf_op jit(solution)/shard_map/ppermute | solution.py:35
  60.2 3.5 %first.1 = (bf16[1024,1536]{1,0:T(8,128)(2,1)S(1)}, bf16[64,1536]{1,0:T(8,128)(2,1)S(1)}, bf16[64,1536]{1,0:T(8,128)(2,1)S(1)}, f32[64,1536]{1,0:T(8,128)S(1)}, ...) custom-call(s32[5]{0:T(128)S(1)} %stack.23.pos, ...), custom_call_target="tpu_custom_call" | custom-call | flops 4831838208 | bytes 1048576 | tf_op jit(solution)/shard_map/first/pallas_call | solution.py:91
  63.8 0.1 fusion.6
  64.0 0.1 collective-permute-start.25
  64.1 1.8 %collective-permute-start.16 = (bf16[64,1536]{1,0:T(8,128)(2,1)S(1)}, bf16[64,1536]{1,0:T(8,128)(2,1)S(1)}, u32[]{:S(2)}, u32[]{:S(2)}) collective-permute-start(bf16[64,1536]{1,0:T(8,128)(2,1)S(1)} %get-tuple-element.83), channel_id=1, source_target_pairs={{0,32},{32,64},{64,96},{96,0},{1,33},{33,65},{65,97},{97,1},{2,34}... | collective-permute-start | bytes 589832 | tf_op jit(solution)/shard_map/ppermute | solution.py:35
  65.8 0.3 collective-permute-start.17
  66.2 0.8 collective-permute-start.19
  67.0 4.4 %collective-permute-done.16 = bf16[64,1536]{1,0:T(8,128)(2,1)S(1)} collective-permute-done((bf16[64,1536]{1,0:T(8,128)(2,1)S(1)}, bf16[64,1536]{1,0:T(8,128)(2,1)S(1)}, u32[]{:S(2)}, u32[]{:S(2)}) %collective-permute-start.16) | collective-permute-done | bytes 196640 | tf_op jit(solution)/shard_map/ppermute | solution.py:35
  71.4 3.4 %collective-permute-done.17 = bf16[64,1536]{1,0:T(8,128)(2,1)S(1)} collective-permute-done((bf16[64,1536]{1,0:T(8,128)(2,1)S(1)}, bf16[64,1536]{1,0:T(8,128)(2,1)S(1)}, u32[]{:S(2)}, u32[]{:S(2)}) %collective-permute-start.17) | collective-permute-done | bytes 196640 | tf_op jit(solution)/shard_map/ppermute | solution.py:35
  74.9 0.6 collective-permute-start.15
  75.5 2.7 %collective-permute-done.19 = bf16[64,1536]{1,0:T(8,128)(2,1)S(1)} collective-permute-done((bf16[64,1536]{1,0:T(8,128)(2,1)S(1)}, bf16[64,1536]{1,0:T(8,128)(2,1)S(1)}, u32[]{:S(2)}, u32[]{:S(2)}) %collective-permute-start.19) | collective-permute-done | bytes 196640 | tf_op jit(solution)/shard_map/ppermute | solution.py:35
  78.2 4.2 %collective-permute-done.18 = bf16[64,1536]{1,0:T(8,128)(2,1)S(1)} collective-permute-done((bf16[64,1536]{1,0:T(8,128)(2,1)S(1)}, bf16[64,1536]{1,0:T(8,128)(2,1)S(1)}, u32[]{:S(2)}, u32[]{:S(2)}) %collective-permute-start.18) | collective-permute-done | bytes 196640 | tf_op jit(solution)/shard_map/ppermute | solution.py:35
  82.6 2.9 %collective-permute-start.21 = (bf16[64,1536]{1,0:T(8,128)(2,1)S(1)}, bf16[64,1536]{1,0:T(8,128)(2,1)S(1)}, u32[]{:S(2)}, u32[]{:S(2)}) collective-permute-start(bf16[64,1536]{1,0:T(8,128)(2,1)S(1)} %add_convert_fusion.4), channel_id=1, source_target_pairs={{0,128},{128,0},{1,129},{129,1},{2,130},{130,2},{3,131},{131,3},{4... | collective-permute-start | bytes 589832 | tf_op jit(solution)/shard_map/ppermute | solution.py:35
  85.5 4.6 %collective-permute-done.20 = bf16[64,1536]{1,0:T(8,128)(2,1)S(1)} collective-permute-done((bf16[64,1536]{1,0:T(8,128)(2,1)S(1)}, bf16[64,1536]{1,0:T(8,128)(2,1)S(1)}, u32[]{:S(2)}, u32[]{:S(2)}) %collective-permute-start.20) | collective-permute-done | bytes 196640 | tf_op jit(solution)/shard_map/ppermute | solution.py:35
  90.1 0.1 multiply_convert_fusion.refs_0_
  90.3 3.2 %collective-permute-start.23 = (bf16[64,1536]{1,0:T(8,128)(2,1)S(1)}, bf16[64,1536]{1,0:T(8,128)(2,1)S(1)}, u32[]{:S(2)}, u32[]{:S(2)}) collective-permute-start(bf16[64,1536]{1,0:T(8,128)(2,1)S(1)} %multiply_convert_fusion.refs_0_), channel_id=1, source_target_pairs={{0,32},{32,64},{64,96},{96,0},{1,33},{33,65},{65,97},{97,1},{2,34}... | collective-permute-start | bytes 589832 | tf_op jit(solution)/shard_map/ppermute | solution.py:35
  93.6 2.9 %collective-permute-start.22 = (bf16[64,1536]{1,0:T(8,128)(2,1)S(1)}, bf16[64,1536]{1,0:T(8,128)(2,1)S(1)}, u32[]{:S(2)}, u32[]{:S(2)}) collective-permute-start(bf16[64,1536]{1,0:T(8,128)(2,1)S(1)} %multiply_convert_fusion.refs_0_), channel_id=1, source_target_pairs={{0,128},{128,0},{1,129},{129,1},{2,130},{130,2},{3,131},{131,3},{4... | collective-permute-start | bytes 589832 | tf_op jit(solution)/shard_map/ppermute | solution.py:35
  96.4 4.9 %wout_grad.1 = bf16[768,1536]{1,0:T(8,128)(2,1)} custom-call(s32[5]{0:T(128)S(1)} %stack.23.pos, s32[6,12]{1,0:T(8,128)S(1)} %copy-done.4, bf16[256,768]{1,0:T(8,128)(2,1)S(1)} %constant_dynamic-update-slice_fusion.4.refs_0_, bf16[256,768]{1,0:T(8,128)(2,1)S(1)} %collective-permute-done.9.refs_1_, bf16[256,768]{1,0:T(8,128)(2,1)S(1)} %collective-permute-done.10.refs_2_, ...), custom_call_target="tpu_custom_call" | custom-call | flops 4831838208 | bytes 8388608 | tf_op jit(solution)/shard_map/wout_grad/pallas_call | solution.py:258
  101.4 3.2 %collective-permute-start.26 = (bf16[64,1536]{1,0:T(8,128)(2,1)S(1)}, bf16[64,1536]{1,0:T(8,128)(2,1)S(1)}, u32[]{:S(2)}, u32[]{:S(2)}) collective-permute-start(bf16[64,1536]{1,0:T(8,128)(2,1)S(1)} %collective-permute-done.22.refs_1_), channel_id=1, source_target_pairs={{0,32},{32,64},{64,96},{96,0},{1,33},{33,65},{65,97},{97,1},{2,34}... | collective-permute-start | bytes 589832 | tf_op jit(solution)/shard_map/ppermute | solution.py:35
  104.6 0.5 collective-permute-start.28
  105.1 3.7 %collective-permute-done.27.refs_5_ = bf16[64,1536]{1,0:T(8,128)(2,1)S(1)} collective-permute-done((bf16[64,1536]{1,0:T(8,128)(2,1)S(1)}, bf16[64,1536]{1,0:T(8,128)(2,1)S(1)}, u32[]{:S(2)}, u32[]{:S(2)}) %collective-permute-start.27) | collective-permute-done | bytes 196640 | tf_op jit(solution)/shard_map/ppermute | solution.py:35
  108.9 1.4 collective-permute-done.28.refs_6_
  110.3 5.5 %collective-permute-done.29.refs_7_ = bf16[64,1536]{1,0:T(8,128)(2,1)S(1)} collective-permute-done((bf16[64,1536]{1,0:T(8,128)(2,1)S(1)}, bf16[64,1536]{1,0:T(8,128)(2,1)S(1)}, u32[]{:S(2)}, u32[]{:S(2)}) %collective-permute-start.29) | collective-permute-done | bytes 196640 | tf_op jit(solution)/shard_map/ppermute | solution.py:35
  115.8 3.4 %second.1 = (bf16[512,768]{1,0:T(8,128)(2,1)S(1)}, bf16[512,768]{1,0:T(8,128)(2,1)S(1)}, bf16[64,1536]{1,0:T(8,128)(2,1)S(1)}, f32[64,1536]{1,0:T(8,128)S(1)}, f...) custom-call(s32[5]{0:T(128)S(1)} %stack.23.pos, ...), custom_call_target="tpu_custom_call" | custom-call | flops 4831838208 | bytes 1048576 | tf_op jit(solution)/shard_map/second/pallas_call | solution.py:91
  119.2 0.1 collective-permute-start.30
  119.2 3.2 %collective-permute-start.32 = (bf16[64,1536]{1,0:T(8,128)(2,1)S(1)}, bf16[64,1536]{1,0:T(8,128)(2,1)S(1)}, u32[]{:S(2)}, u32[]{:S(2)}) collective-permute-start(bf16[64,1536]{1,0:T(8,128)(2,1)S(1)} %get-tuple-element.107), channel_id=1, source_target_pairs={{0,28},{4,0},{8,4},{12,8},{16,12},{20,16},{24,20},{28,24},{1,29},{... | collective-permute-start | bytes 589832 | tf_op jit(solution)/shard_map/ppermute | solution.py:35
  122.5 3.6 %collective-permute-done.30 = bf16[64,1536]{1,0:T(8,128)(2,1)S(1)} collective-permute-done((bf16[64,1536]{1,0:T(8,128)(2,1)S(1)}, bf16[64,1536]{1,0:T(8,128)(2,1)S(1)}, u32[]{:S(2)}, u32[]{:S(2)}) %collective-permute-start.30) | collective-permute-done | bytes 196640 | tf_op jit(solution)/shard_map/ppermute | solution.py:35
  126.1 0.1 collective-permute-start.31
  126.3 3.3 %collective-permute-start.33 = (bf16[64,1536]{1,0:T(8,128)(2,1)S(1)}, bf16[64,1536]{1,0:T(8,128)(2,1)S(1)}, u32[]{:S(2)}, u32[]{:S(2)}) collective-permute-start(bf16[64,1536]{1,0:T(8,128)(2,1)S(1)} %add_convert_fusion.2), channel_id=1, source_target_pairs={{0,28},{4,0},{8,4},{12,8},{16,12},{20,16},{24,20},{28,24},{1,29},{... | collective-permute-start | bytes 589832 | tf_op jit(solution)/shard_map/ppermute | solution.py:35
  129.6 4.8 %win_grad.1 = bf16[1536,768]{1,0:T(8,128)(2,1)} custom-call(s32[12,6]{1,0:T(8,128)S(1)} %copy.10.mask_in.mask, bf16[1024,1536]{1,0:T(8,128)(2,1)S(1)} %get-tuple-element.97.refs_4_.left0, bf16[1024,1536]{1,0:T(8,128)(2,1)S(1)} %collective-permute-done.25.refs_5_.left1, bf16[512,768]{1,0:T(8,128)(2,1)S(1)} %get-tuple-element.108.own, ...), custom_call_target="tpu_custom_call" | custom-call | flops 4831838208 | bytes 8388608 | tf_op jit(solution)/shard_map/win_grad/pallas_call | solution.py:286
  134.4 2.7 %collective-permute-start.35 = (bf16[64,1536]{1,0:T(8,128)(2,1)S(1)}, bf16[64,1536]{1,0:T(8,128)(2,1)S(1)}, u32[]{:S(2)}, u32[]{:S(2)}) collective-permute-start(bf16[64,1536]{1,0:T(8,128)(2,1)S(1)} %add_convert_fusion.1), channel_id=1, source_target_pairs={{0,28},{4,0},{8,4},{12,8},{16,12},{20,16},{24,20},{28,24},{1,29},{... | collective-permute-start | bytes 589832 | tf_op jit(solution)/shard_map/ppermute | solution.py:35
  137.3 4.1 %collective-permute-done.35 = bf16[64,1536]{1,0:T(8,128)(2,1)S(1)} collective-permute-done((bf16[64,1536]{1,0:T(8,128)(2,1)S(1)}, bf16[64,1536]{1,0:T(8,128)(2,1)S(1)}, u32[]{:S(2)}, u32[]{:S(2)}) %collective-permute-start.35) | collective-permute-done | bytes 196640 | tf_op jit(solution)/shard_map/ppermute | solution.py:35
  141.4 3.8 %collective-permute-start.38 = (bf16[32,1536]{1,0:T(8,128)(2,1)S(1)}, bf16[32,1536]{1,0:T(8,128)(2,1)S(1)}, u32[]{:S(2)}, u32[]{:S(2)}) collective-permute-start(bf16[32,1536]{1,0:T(8,128)(2,1)S(1)} %add_convert_fusion.9), channel_id=1, source_target_pairs={{0,28},{4,0},{8,4},{12,8},{16,12},{20,16},{24,20},{28,24},{1,29},{... | collective-permute-start | bytes 294920 | tf_op jit(solution)/shard_map/ppermute | solution.py:35
  145.2 2.2 %collective-permute-done.38 = bf16[32,1536]{1,0:T(8,128)(2,1)S(1)} collective-permute-done((bf16[32,1536]{1,0:T(8,128)(2,1)S(1)}, bf16[32,1536]{1,0:T(8,128)(2,1)S(1)}, u32[]{:S(2)}, u32[]{:S(2)}) %collective-permute-start.38) | collective-permute-done | bytes 98336 | tf_op jit(solution)/shard_map/ppermute | solution.py:35
  147.5 0.9 collective-permute-start.39
  148.4 5.3 %collective-permute-done.37 = bf16[32,1536]{1,0:T(8,128)(2,1)S(1)} collective-permute-done((bf16[32,1536]{1,0:T(8,128)(2,1)S(1)}, bf16[32,1536]{1,0:T(8,128)(2,1)S(1)}, u32[]{:S(2)}, u32[]{:S(2)}) %collective-permute-start.37) | collective-permute-done | bytes 98336 | tf_op jit(solution)/shard_map/ppermute | solution.py:35
  153.7 0.7 add_convert_fusion.7
  (55 shorter events, 1.1 us)
Async XLA Ops:
  0.6 5.8 %collective-permute-start.1 = (bf16[32,1536]{1,0:T(8,128)(2,1)}, bf16[32,1536]{1,0:T(8,128)(2,1)S(1)}, u32[]{:S(2)}, u32[]{:S(2)}) collective-permute-start(bf16[32,1536]{1,0:T(8,128)(2,1)} %param.7), channel_id=1, source_target_pairs={{0,2},{2,0},{1,3},{3,1},{4,6},{6,4},{5,7},{7,5},{8,10},{10,8},{9,1... | collective-permute-start | bytes 294920 | tf_op jit(solution)/shard_map/ppermute | solution.py:35
  2.3 5.4 %collective-permute-start = (bf16[32,1536]{1,0:T(8,128)(2,1)}, bf16[32,1536]{1,0:T(8,128)(2,1)S(1)}, u32[]{:S(2)}, u32[]{:S(2)}) collective-permute-start(bf16[32,1536]{1,0:T(8,128)(2,1)} %param.8), channel_id=1, source_target_pairs={{0,2},{2,0},{1,3},{3,1},{4,6},{6,4},{5,7},{7,5},{8,10},{10,8},{9,1... | collective-permute-start | bytes 294920 | tf_op jit(solution)/shard_map/ppermute | solution.py:35
  3.8 0.9 copy-start.2
  8.6 16.0 %collective-permute-start.3 = (bf16[128,1536]{1,0:T(8,128)(2,1)S(1)}, bf16[128,1536]{1,0:T(8,128)(2,1)S(1)}, u32[]{:S(2)}, u32[]{:S(2)}) collective-permute-start(bf16[128,1536]{1,0:T(8,128)(2,1)S(1)} %constant_dynamic-update-slice_fusion.refs_0_), channel_id=1, source_target_pairs={{0,28},{4,0},{8,4},{12,8},{16,12},{20,16},{24,20},{28,24},{1,29},{... | collective-permute-start | bytes 1179656 | tf_op jit(solution)/shard_map/ppermute | solution.py:35
  14.5 11.2 %collective-permute-start.2 = (bf16[128,1536]{1,0:T(8,128)(2,1)S(1)}, bf16[128,1536]{1,0:T(8,128)(2,1)S(1)}, u32[]{:S(2)}, u32[]{:S(2)}) collective-permute-start(bf16[128,1536]{1,0:T(8,128)(2,1)S(1)} %constant_dynamic-update-slice_fusion.refs_0_), channel_id=1, source_target_pairs={{0,4},{4,8},{8,12},{12,16},{16,20},{20,24},{24,28},{28,0},{1,5},{5... | collective-permute-start | bytes 1179656 | tf_op jit(solution)/shard_map/ppermute | solution.py:35
  14.5 10.1 %collective-permute-start.4 = (bf16[128,768]{1,0:T(8,128)(2,1)S(1)}, bf16[128,768]{1,0:T(8,128)(2,1)S(1)}, u32[]{:S(2)}, u32[]{:S(2)}) collective-permute-start(bf16[128,768]{1,0:T(8,128)(2,1)S(1)} %get-tuple-element.70), channel_id=1, source_target_pairs={{0,128},{128,0},{1,129},{129,1},{2,130},{130,2},{3,131},{131,3},{4... | collective-permute-start | bytes 589832 | tf_op jit(solution)/shard_map/ppermute | solution.py:35
  18.4 1.7 %copy-start = (bf16[768,1536]{1,0:T(8,128)(2,1)S(1)}, bf16[768,1536]{1,0:T(8,128)(2,1)}, u32[]{:S(2)}) copy-start(bf16[768,1536]{1,0:T(8,128)(2,1)} %w_out.1) | copy-start | bytes 7077892
  20.1 1.7 %copy-start.1 = (bf16[1536,768]{1,0:T(8,128)(2,1)S(1)}, bf16[1536,768]{1,0:T(8,128)(2,1)}, u32[]{:S(2)}) copy-start(bf16[1536,768]{1,0:T(8,128)(2,1)} %w_in.1) | copy-start | bytes 7077892
  21.7 0.7 copy-start.3
  25.7 34.6 %collective-permute-start.14 = (bf16[1600,1536]{1,0:T(8,128)(2,1)S(1)}, bf16[1600,1536]{1,0:T(8,128)(2,1)S(1)}, u32[]{:S(2)}, u32[]{:S(2)}) collective-permute-start(bf16[1600,1536]{1,0:T(8,128)(2,1)S(1)} %masked.1.refs_9_.refs_8_), channel_id=1, source_target_pairs={{0,1},{1,0},{2,3},{3,2},{4,5},{5,4},{6,7},{7,6},{8,9},{9,8},{10,11... | collective-permute-start | bytes 14745608 | tf_op jit(solution)/shard_map/ppermute | solution.py:35
  25.7 12.7 %collective-permute-start.5 = (bf16[128,1536]{1,0:T(8,128)(2,1)S(1)}, bf16[128,1536]{1,0:T(8,128)(2,1)S(1)}, u32[]{:S(2)}, u32[]{:S(2)}) collective-permute-start(bf16[128,1536]{1,0:T(8,128)(2,1)S(1)} %collective-permute-done.2.refs_1_), channel_id=1, source_target_pairs={{0,4},{4,8},{8,12},{12,16},{16,20},{20,24},{24,28},{28,0},{1,5},{5... | collective-permute-start | bytes 1179656 | tf_op jit(solution)/shard_map/ppermute | solution.py:35
  25.7 12.7 %collective-permute-start.6 = (bf16[128,1536]{1,0:T(8,128)(2,1)S(1)}, bf16[128,1536]{1,0:T(8,128)(2,1)S(1)}, u32[]{:S(2)}, u32[]{:S(2)}) collective-permute-start(bf16[128,1536]{1,0:T(8,128)(2,1)S(1)} %collective-permute-done.3.refs_2_), channel_id=1, source_target_pairs={{0,28},{4,0},{8,4},{12,8},{16,12},{20,16},{24,20},{28,24},{1,29},{... | collective-permute-start | bytes 1179656 | tf_op jit(solution)/shard_map/ppermute | solution.py:35
  29.0 12.7 %collective-permute-start.10 = (bf16[256,768]{1,0:T(8,128)(2,1)S(1)}, bf16[256,768]{1,0:T(8,128)(2,1)S(1)}, u32[]{:S(2)}, u32[]{:S(2)}) collective-permute-start(bf16[256,768]{1,0:T(8,128)(2,1)S(1)} %constant_dynamic-update-slice_fusion.4.refs_0_), channel_id=1, source_target_pairs={{0,96},{32,0},{64,32},{96,64},{1,97},{33,1},{65,33},{97,65},{2,98}... | collective-permute-start | bytes 1179656 | tf_op jit(solution)/shard_map/ppermute | solution.py:35
  29.9 11.8 %collective-permute-start.9 = (bf16[256,768]{1,0:T(8,128)(2,1)S(1)}, bf16[256,768]{1,0:T(8,128)(2,1)S(1)}, u32[]{:S(2)}, u32[]{:S(2)}) collective-permute-start(bf16[256,768]{1,0:T(8,128)(2,1)S(1)} %constant_dynamic-update-slice_fusion.4.refs_0_), channel_id=1, source_target_pairs={{0,32},{32,64},{64,96},{96,0},{1,33},{33,65},{65,97},{97,1},{2,34}... | collective-permute-start | bytes 1179656 | tf_op jit(solution)/shard_map/ppermute | solution.py:35
  38.4 12.0 %collective-permute-start.7 = (bf16[128,1536]{1,0:T(8,128)(2,1)S(1)}, bf16[128,1536]{1,0:T(8,128)(2,1)S(1)}, u32[]{:S(2)}, u32[]{:S(2)}) collective-permute-start(bf16[128,1536]{1,0:T(8,128)(2,1)S(1)} %collective-permute-done.5.refs_3_), channel_id=1, source_target_pairs={{0,4},{4,8},{8,12},{12,16},{16,20},{20,24},{24,28},{28,0},{1,5},{5... | collective-permute-start | bytes 1179656 | tf_op jit(solution)/shard_map/ppermute | solution.py:35
  38.4 12.0 %collective-permute-start.8 = (bf16[128,1536]{1,0:T(8,128)(2,1)S(1)}, bf16[128,1536]{1,0:T(8,128)(2,1)S(1)}, u32[]{:S(2)}, u32[]{:S(2)}) collective-permute-start(bf16[128,1536]{1,0:T(8,128)(2,1)S(1)} %collective-permute-done.6.refs_4_), channel_id=1, source_target_pairs={{0,28},{4,0},{8,4},{12,8},{16,12},{20,16},{24,20},{28,24},{1,29},{... | collective-permute-start | bytes 1179656 | tf_op jit(solution)/shard_map/ppermute | solution.py:35
  50.4 9.9 %collective-permute-start.13 = (bf16[256,768]{1,0:T(8,128)(2,1)S(1)}, bf16[256,768]{1,0:T(8,128)(2,1)S(1)}, u32[]{:S(2)}, u32[]{:S(2)}) collective-permute-start(bf16[256,768]{1,0:T(8,128)(2,1)S(1)} %collective-permute-done.9.refs_1_), channel_id=1, source_target_pairs={{0,32},{32,64},{64,96},{96,0},{1,33},{33,65},{65,97},{97,1},{2,34}... | collective-permute-start | bytes 1179656 | tf_op jit(solution)/shard_map/ppermute | solution.py:35
  50.9 7.0 %collective-permute-start.11 = (bf16[64,1536]{1,0:T(8,128)(2,1)S(1)}, bf16[64,1536]{1,0:T(8,128)(2,1)S(1)}, u32[]{:S(2)}, u32[]{:S(2)}) collective-permute-start(bf16[64,1536]{1,0:T(8,128)(2,1)S(1)} %slice.27), channel_id=1, source_target_pairs={{0,4},{4,8},{8,12},{12,16},{16,20},{20,24},{24,28},{28,0},{1,5},{5... | collective-permute-start | bytes 589832 | tf_op jit(solution)/shard_map/ppermute | solution.py:35
  51.1 6.7 %collective-permute-start.12 = (bf16[64,1536]{1,0:T(8,128)(2,1)S(1)}, bf16[64,1536]{1,0:T(8,128)(2,1)S(1)}, u32[]{:S(2)}, u32[]{:S(2)}) collective-permute-start(bf16[64,1536]{1,0:T(8,128)(2,1)S(1)} %slice.28), channel_id=1, source_target_pairs={{0,28},{4,0},{8,4},{12,8},{16,12},{20,16},{24,20},{28,24},{1,29},{... | collective-permute-start | bytes 589832 | tf_op jit(solution)/shard_map/ppermute | solution.py:35
  63.8 32.6 %copy-start.4 = (s32[6,12]{1,0:T(8,128)S(1)}, s32[6,12]{1,0:T(8,128)}, u32[]{:S(2)}) copy-start(s32[6,12]{1,0:T(8,128)} %mask.2) | copy-start | bytes 868
  64.0 32.4 %collective-permute-start.25 = (bf16[1024,1536]{1,0:T(8,128)(2,1)S(1)}, bf16[1024,1536]{1,0:T(8,128)(2,1)S(1)}, u32[]{:S(2)}, u32[]{:S(2)}) collective-permute-start(bf16[1024,1536]{1,0:T(8,128)(2,1)S(1)} %get-tuple-element.97.refs_4_.left0), channel_id=1, source_target_pairs={{0,1},{1,0},{2,3},{3,2},{4,5},{5,4},{6,7},{7,6},{8,9},{9,8},{10,11... | collective-permute-start | bytes 9437192 | tf_op jit(solution)/shard_map/ppermute | solution.py:35
  64.1 7.3 %collective-permute-start.16 = (bf16[64,1536]{1,0:T(8,128)(2,1)S(1)}, bf16[64,1536]{1,0:T(8,128)(2,1)S(1)}, u32[]{:S(2)}, u32[]{:S(2)}) collective-permute-start(bf16[64,1536]{1,0:T(8,128)(2,1)S(1)} %get-tuple-element.83), channel_id=1, source_target_pairs={{0,32},{32,64},{64,96},{96,0},{1,33},{33,65},{65,97},{97,1},{2,34}... | collective-permute-start | bytes 589832 | tf_op jit(solution)/shard_map/ppermute | solution.py:35
  65.8 9.0 %collective-permute-start.17 = (bf16[64,1536]{1,0:T(8,128)(2,1)S(1)}, bf16[64,1536]{1,0:T(8,128)(2,1)S(1)}, u32[]{:S(2)}, u32[]{:S(2)}) collective-permute-start(bf16[64,1536]{1,0:T(8,128)(2,1)S(1)} %get-tuple-element.84), channel_id=1, source_target_pairs={{0,96},{32,0},{64,32},{96,64},{1,97},{33,1},{65,33},{97,65},{2,98}... | collective-permute-start | bytes 589832 | tf_op jit(solution)/shard_map/ppermute | solution.py:35
  66.2 12.0 %collective-permute-start.19 = (bf16[64,1536]{1,0:T(8,128)(2,1)S(1)}, bf16[64,1536]{1,0:T(8,128)(2,1)S(1)}, u32[]{:S(2)}, u32[]{:S(2)}) collective-permute-start(bf16[64,1536]{1,0:T(8,128)(2,1)S(1)} %get-tuple-element.89), channel_id=1, source_target_pairs={{0,96},{32,0},{64,32},{96,64},{1,97},{33,1},{65,33},{97,65},{2,98}... | collective-permute-start | bytes 589832 | tf_op jit(solution)/shard_map/ppermute | solution.py:35
  74.9 7.5 %collective-permute-start.18 = (bf16[64,1536]{1,0:T(8,128)(2,1)S(1)}, bf16[64,1536]{1,0:T(8,128)(2,1)S(1)}, u32[]{:S(2)}, u32[]{:S(2)}) collective-permute-start(bf16[64,1536]{1,0:T(8,128)(2,1)S(1)} %add_convert_fusion.6), channel_id=1, source_target_pairs={{0,32},{32,64},{64,96},{96,0},{1,33},{33,65},{65,97},{97,1},{2,34}... | collective-permute-start | bytes 589832 | tf_op jit(solution)/shard_map/ppermute | solution.py:35
  74.9 10.6 %collective-permute-start.15 = (bf16[64,1536]{1,0:T(8,128)(2,1)S(1)}, bf16[64,1536]{1,0:T(8,128)(2,1)S(1)}, u32[]{:S(2)}, u32[]{:S(2)}) collective-permute-start(bf16[64,1536]{1,0:T(8,128)(2,1)S(1)} %get-tuple-element.80), channel_id=1, source_target_pairs={{0,32},{32,64},{64,96},{96,0},{1,33},{33,65},{65,97},{97,1},{2,34}... | collective-permute-start | bytes 589832 | tf_op jit(solution)/shard_map/ppermute | solution.py:35
  82.4 7.7 %collective-permute-start.20 = (bf16[64,1536]{1,0:T(8,128)(2,1)S(1)}, bf16[64,1536]{1,0:T(8,128)(2,1)S(1)}, u32[]{:S(2)}, u32[]{:S(2)}) collective-permute-start(bf16[64,1536]{1,0:T(8,128)(2,1)S(1)} %add_convert_fusion.5), channel_id=1, source_target_pairs={{0,96},{32,0},{64,32},{96,64},{1,97},{33,1},{65,33},{97,65},{2,98}... | collective-permute-start | bytes 589832 | tf_op jit(solution)/shard_map/ppermute | solution.py:35
  82.6 7.5 %collective-permute-start.21 = (bf16[64,1536]{1,0:T(8,128)(2,1)S(1)}, bf16[64,1536]{1,0:T(8,128)(2,1)S(1)}, u32[]{:S(2)}, u32[]{:S(2)}) collective-permute-start(bf16[64,1536]{1,0:T(8,128)(2,1)S(1)} %add_convert_fusion.4), channel_id=1, source_target_pairs={{0,128},{128,0},{1,129},{129,1},{2,130},{130,2},{3,131},{131,3},{4... | collective-permute-start | bytes 589832 | tf_op jit(solution)/shard_map/ppermute | solution.py:35
  90.2 11.0 %collective-permute-start.24 = (bf16[64,1536]{1,0:T(8,128)(2,1)S(1)}, bf16[64,1536]{1,0:T(8,128)(2,1)S(1)}, u32[]{:S(2)}, u32[]{:S(2)}) collective-permute-start(bf16[64,1536]{1,0:T(8,128)(2,1)S(1)} %multiply_convert_fusion.refs_0_), channel_id=1, source_target_pairs={{0,96},{32,0},{64,32},{96,64},{1,97},{33,1},{65,33},{97,65},{2,98}... | collective-permute-start | bytes 589832 | tf_op jit(solution)/shard_map/ppermute | solution.py:35
  90.3 10.9 %collective-permute-start.23 = (bf16[64,1536]{1,0:T(8,128)(2,1)S(1)}, bf16[64,1536]{1,0:T(8,128)(2,1)S(1)}, u32[]{:S(2)}, u32[]{:S(2)}) collective-permute-start(bf16[64,1536]{1,0:T(8,128)(2,1)S(1)} %multiply_convert_fusion.refs_0_), channel_id=1, source_target_pairs={{0,32},{32,64},{64,96},{96,0},{1,33},{33,65},{65,97},{97,1},{2,34}... | collective-permute-start | bytes 589832 | tf_op jit(solution)/shard_map/ppermute | solution.py:35
  93.6 7.7 %collective-permute-start.22 = (bf16[64,1536]{1,0:T(8,128)(2,1)S(1)}, bf16[64,1536]{1,0:T(8,128)(2,1)S(1)}, u32[]{:S(2)}, u32[]{:S(2)}) collective-permute-start(bf16[64,1536]{1,0:T(8,128)(2,1)S(1)} %multiply_convert_fusion.refs_0_), channel_id=1, source_target_pairs={{0,128},{128,0},{1,129},{129,1},{2,130},{130,2},{3,131},{131,3},{4... | collective-permute-start | bytes 589832 | tf_op jit(solution)/shard_map/ppermute | solution.py:35
  101.3 7.6 %collective-permute-start.27 = (bf16[64,1536]{1,0:T(8,128)(2,1)S(1)}, bf16[64,1536]{1,0:T(8,128)(2,1)S(1)}, u32[]{:S(2)}, u32[]{:S(2)}) collective-permute-start(bf16[64,1536]{1,0:T(8,128)(2,1)S(1)} %collective-permute-done.22.refs_1_), channel_id=1, source_target_pairs={{0,96},{32,0},{64,32},{96,64},{1,97},{33,1},{65,33},{97,65},{2,98}... | collective-permute-start | bytes 589832 | tf_op jit(solution)/shard_map/ppermute | solution.py:35
  101.4 8.9 %collective-permute-start.26 = (bf16[64,1536]{1,0:T(8,128)(2,1)S(1)}, bf16[64,1536]{1,0:T(8,128)(2,1)S(1)}, u32[]{:S(2)}, u32[]{:S(2)}) collective-permute-start(bf16[64,1536]{1,0:T(8,128)(2,1)S(1)} %collective-permute-done.22.refs_1_), channel_id=1, source_target_pairs={{0,32},{32,64},{64,96},{96,0},{1,33},{33,65},{65,97},{97,1},{2,34}... | collective-permute-start | bytes 589832 | tf_op jit(solution)/shard_map/ppermute | solution.py:35
  104.6 5.7 %collective-permute-start.28 = (bf16[64,1536]{1,0:T(8,128)(2,1)S(1)}, bf16[64,1536]{1,0:T(8,128)(2,1)S(1)}, u32[]{:S(2)}, u32[]{:S(2)}) collective-permute-start(bf16[64,1536]{1,0:T(8,128)(2,1)S(1)} %collective-permute-done.23.refs_2_), channel_id=1, source_target_pairs={{0,32},{32,64},{64,96},{96,0},{1,33},{33,65},{65,97},{97,1},{2,34}... | collective-permute-start | bytes 589832 | tf_op jit(solution)/shard_map/ppermute | solution.py:35
  108.9 6.9 %collective-permute-start.29 = (bf16[64,1536]{1,0:T(8,128)(2,1)S(1)}, bf16[64,1536]{1,0:T(8,128)(2,1)S(1)}, u32[]{:S(2)}, u32[]{:S(2)}) collective-permute-start(bf16[64,1536]{1,0:T(8,128)(2,1)S(1)} %collective-permute-done.27.refs_5_), channel_id=1, source_target_pairs={{0,96},{32,0},{64,32},{96,64},{1,97},{33,1},{65,33},{97,65},{2,98}... | collective-permute-start | bytes 589832 | tf_op jit(solution)/shard_map/ppermute | solution.py:35
  119.2 7.0 %collective-permute-start.30 = (bf16[64,1536]{1,0:T(8,128)(2,1)S(1)}, bf16[64,1536]{1,0:T(8,128)(2,1)S(1)}, u32[]{:S(2)}, u32[]{:S(2)}) collective-permute-start(bf16[64,1536]{1,0:T(8,128)(2,1)S(1)} %get-tuple-element.105), channel_id=1, source_target_pairs={{0,4},{4,8},{8,12},{12,16},{16,20},{20,24},{24,28},{28,0},{1,5},{5... | collective-permute-start | bytes 589832 | tf_op jit(solution)/shard_map/ppermute | solution.py:35
  119.2 7.0 %collective-permute-start.32 = (bf16[64,1536]{1,0:T(8,128)(2,1)S(1)}, bf16[64,1536]{1,0:T(8,128)(2,1)S(1)}, u32[]{:S(2)}, u32[]{:S(2)}) collective-permute-start(bf16[64,1536]{1,0:T(8,128)(2,1)S(1)} %get-tuple-element.107), channel_id=1, source_target_pairs={{0,28},{4,0},{8,4},{12,8},{16,12},{20,16},{24,20},{28,24},{1,29},{... | collective-permute-start | bytes 589832 | tf_op jit(solution)/shard_map/ppermute | solution.py:35
  122.5 7.1 %collective-permute-start.34 = (bf16[512,768]{1,0:T(8,128)(2,1)S(1)}, bf16[512,768]{1,0:T(8,128)(2,1)S(1)}, u32[]{:S(2)}, u32[]{:S(2)}) collective-permute-start(bf16[512,768]{1,0:T(8,128)(2,1)S(1)} %get-tuple-element.109), channel_id=1, source_target_pairs={{0,1},{1,0},{2,3},{3,2},{4,5},{5,4},{6,7},{7,6},{8,9},{9,8},{10,11... | collective-permute-start | bytes 2359304 | tf_op jit(solution)/shard_map/ppermute | solution.py:35
  126.1 8.2 %collective-permute-start.31 = (bf16[64,1536]{1,0:T(8,128)(2,1)S(1)}, bf16[64,1536]{1,0:T(8,128)(2,1)S(1)}, u32[]{:S(2)}, u32[]{:S(2)}) collective-permute-start(bf16[64,1536]{1,0:T(8,128)(2,1)S(1)} %add_convert_fusion.3), channel_id=1, source_target_pairs={{0,4},{4,8},{8,12},{12,16},{16,20},{20,24},{24,28},{28,0},{1,5},{5... | collective-permute-start | bytes 589832 | tf_op jit(solution)/shard_map/ppermute | solution.py:35
  126.3 8.1 %collective-permute-start.33 = (bf16[64,1536]{1,0:T(8,128)(2,1)S(1)}, bf16[64,1536]{1,0:T(8,128)(2,1)S(1)}, u32[]{:S(2)}, u32[]{:S(2)}) collective-permute-start(bf16[64,1536]{1,0:T(8,128)(2,1)S(1)} %add_convert_fusion.2), channel_id=1, source_target_pairs={{0,28},{4,0},{8,4},{12,8},{16,12},{20,16},{24,20},{28,24},{1,29},{... | collective-permute-start | bytes 589832 | tf_op jit(solution)/shard_map/ppermute | solution.py:35
  134.4 7.0 %collective-permute-start.35 = (bf16[64,1536]{1,0:T(8,128)(2,1)S(1)}, bf16[64,1536]{1,0:T(8,128)(2,1)S(1)}, u32[]{:S(2)}, u32[]{:S(2)}) collective-permute-start(bf16[64,1536]{1,0:T(8,128)(2,1)S(1)} %add_convert_fusion.1), channel_id=1, source_target_pairs={{0,28},{4,0},{8,4},{12,8},{16,12},{20,16},{24,20},{28,24},{1,29},{... | collective-permute-start | bytes 589832 | tf_op jit(solution)/shard_map/ppermute | solution.py:35
  137.2 8.0 %collective-permute-start.36 = (bf16[64,1536]{1,0:T(8,128)(2,1)S(1)}, bf16[64,1536]{1,0:T(8,128)(2,1)S(1)}, u32[]{:S(2)}, u32[]{:S(2)}) collective-permute-start(bf16[64,1536]{1,0:T(8,128)(2,1)S(1)} %add_convert_fusion), channel_id=1, source_target_pairs={{0,4},{4,8},{8,12},{12,16},{16,20},{20,24},{24,28},{28,0},{1,5},{5... | collective-permute-start | bytes 589832 | tf_op jit(solution)/shard_map/ppermute | solution.py:35
  141.4 6.0 %collective-permute-start.38 = (bf16[32,1536]{1,0:T(8,128)(2,1)S(1)}, bf16[32,1536]{1,0:T(8,128)(2,1)S(1)}, u32[]{:S(2)}, u32[]{:S(2)}) collective-permute-start(bf16[32,1536]{1,0:T(8,128)(2,1)S(1)} %add_convert_fusion.9), channel_id=1, source_target_pairs={{0,28},{4,0},{8,4},{12,8},{16,12},{20,16},{24,20},{28,24},{1,29},{... | collective-permute-start | bytes 294920 | tf_op jit(solution)/shard_map/ppermute | solution.py:35
  147.4 6.3 %collective-permute-start.37 = (bf16[32,1536]{1,0:T(8,128)(2,1)S(1)}, bf16[32,1536]{1,0:T(8,128)(2,1)S(1)}, u32[]{:S(2)}, u32[]{:S(2)}) collective-permute-start(bf16[32,1536]{1,0:T(8,128)(2,1)S(1)} %get-tuple-element.117), channel_id=1, source_target_pairs={{0,4},{4,8},{8,12},{12,16},{16,20},{20,24},{24,28},{28,0},{1,5},{5... | collective-permute-start | bytes 294920 | tf_op jit(solution)/shard_map/ppermute | solution.py:35
  147.5 6.2 %collective-permute-start.39 = (bf16[32,1536]{1,0:T(8,128)(2,1)S(1)}, bf16[32,1536]{1,0:T(8,128)(2,1)S(1)}, u32[]{:S(2)}, u32[]{:S(2)}) collective-permute-start(bf16[32,1536]{1,0:T(8,128)(2,1)S(1)} %get-tuple-element.118), channel_id=1, source_target_pairs={{0,2},{2,0},{1,3},{3,1},{4,6},{6,4},{5,7},{7,5},{8,10},{10,8},{9,1... | collective-permute-start | bytes 294920 | tf_op jit(solution)/shard_map/ppermute | solution.py:35
where the time goes:
time: 155 us; the launch traced here: 154 us
  waiting for transfers between devices  69.3 us (45%)
  starting transfers between devices  55.6 us (36%)
  Pallas kernels  19.5 us (13%)
  local copies, waits for them, and re-layouts  7.71 us (5%)
    ppermute x40, waiting for transfers between devices, shift(): lax.ppermute(value, axis, [(i, (i + by) % count) for i in range(count)])  69.3 us
    ppermute x40, starting transfers between devices, shift(): lax.ppermute(value, axis, [(i, (i + by) % count) for i in range(count)])  55.6 us
    pallas_call x3, Pallas kernels, call(): pl.pallas_call(kernel, in_specs=[pl.BlockSpec(memory_space=pltpu.SMEM)] +...  7.74 us
    unnamed x15, local copies, waits for them, and re-layouts  7.58 us
    pallas_call x1, Pallas kernels, wout_grad(): pl.pallas_call(functools.partial(wout_kernel, plan_x(128)), grid_spec=plt...  4.85 us
    pallas_call x1, Pallas kernels, win_grad(): pl.pallas_call(win_kernel, grid_spec=pltpu.PrefetchScalarGridSpec(num_sca...  4.79 us
  transfers between devices with their start and end apart: 40, of which 19 were waited for; matrix products, arithmetic and copies ran while one was open for 1% of the time, Pallas kernels for 8%

commit v1 on v0

--- a/solution.py
+++ b/solution.py
@@ -55,13 +55,12 @@
     return shift(up, axis, 1), shift(down, axis, -1)
 
 
-def plan_z(count):
-    half = lambda off, kind, at: [(at, off, 0, kind), (at + count, off, 1, kind)]
-    both = lambda off: half(off, 0, 0) + half(off, 1, 2 * count)
+def plan_z():
+    both = lambda off: [(0, off, 0), (32, off, 1), (64, off, 2)]
     plan = [both(0)]
     for step in range(1, 4):
         plan += [both(-step), both(step)]
-    return plan + [half(4, 0, 0), half(4, 1, 0)]
+    return plan + [[(0, 4, 0), (32, 4, 1)], [(0, 4, 2)]]
 
 
 def plan_x(count):
@@ -73,14 +72,14 @@
     return pl.BlockSpec(shape, lambda *_: (0,) * len(shape))
 
 
-def place_z(pos, off, half, count):
+def place_z(pos, off, half):
     owner = lax.rem(pos[2] + (off + 8), 8)
-    return pl.multiple_of(owner * (2 * count) + lax.rem(pos[3] + half, 2) * count, 16)
-
-
-def place_x(pos, off, half, count):
-    owner = lax.rem(pos[0] + half, 2) * 4 + lax.rem(pos[1] + (off + 4), 4)
-    return pl.multiple_of(owner * count, 16)
+    return pl.ds(pl.multiple_of(half * 256 + owner * 32, 32), 32)
+
+
+def place_x(pos, off, y):
+    owner = lax.rem(pos[0] + y, 2) * 4 + lax.rem(pos[1] + (off + 4), 4)
+    return [pl.ds(pl.multiple_of(half * 256 + owner * 32, 32), 32) for half in range(2)]
 
 
 def in_vmem(count):
@@ -139,94 +138,96 @@
     tval = jnp.tanh(coef * (zval + 0.044715 * zval**3))
     hidden[...] = (0.5 * zval * (1.0 + tval)).astype(BF)
     for half in range(2):
-        mine = pl.ds(pl.multiple_of(half * 64 + core * 32, 32), 32)
-        theirs = pl.ds(pl.multiple_of(half * 64 + (1 - core) * 32, 32), 32)
+        first = lax.rem(pos[3] + half, 2) * 64
+        mine = pl.ds(pl.multiple_of(first + core * 32, 32), 32)
+        theirs = pl.ds(pl.multiple_of(first + (1 - core) * 32, 32), 32)
         rows = slice(half * 32, half * 32 + 32)
         slopes[rows, :] = slope(pre[mine, :])
         other[rows, :] = pre[theirs, :]
 
 
-def first_kernel(plan, count, pos, *refs):
+def first_kernel(plan, pos, *refs):
     pieces = refs[: len(plan)]
-    own_ref, peer_ref, rows = refs[len(plan) : len(plan) + 3]
-    outs, held = refs[len(plan) + 3 : -1], refs[-1]
-    two = 2 * count
+    own_ref, peer_ref, rows, ins = refs[len(plan) : len(plan) + 4]
+    outs, held = refs[len(plan) + 4 : -1], refs[-1]
     for ref, spots in zip(pieces, plan):
-        for first, off, half, kind in spots:
-            at = pl.ds(place_z(pos, off, half, count) + kind * 16 * count, count)
-            rows[at, :] = ref[first : first + count, :]
+        for first, off, half in spots:
+            rows[place_z(pos, off, half), :] = ref[first : first + 32, :]
+            if half == 2:
+                ins[place_z(pos, off, 0), :] = ref[first : first + 32, :]
 
     for half, weight in enumerate((own_ref, peer_ref)):
         held[...] = lax.dot_general(
-            rows[0 : 16 * count, :], weight[0:768, :], NT, preferred_element_type=F32
+            rows[0:512, :], weight[0:768, :], NT, preferred_element_type=F32
         )
         where = slice(half * 768, half * 768 + 768)
 
         for ref, (off, y, _) in zip(outs, TO_X):
-            block = held[pl.ds(place_x(pos, off, y, two), two), :]
-            ref[:, where] = block.astype(ref.dtype)
-
-
-def first(pos, pieces, own, peer, count):
-    tokens, two = 16 * count, 2 * count
-    heights = [(2 * tokens, BF)] + [(two, kind) for _, _, kind in TO_X]
+            for k, place in enumerate(place_x(pos, off, y)):
+                ref[k * 32 : k * 32 + 32, where] = held[place, :].astype(ref.dtype)
+
+
+def first(pos, pieces, own, peer):
+    heights = [(768, BF), (256, BF)] + [(64, kind) for _, _, kind in TO_X]
     return call(
-        functools.partial(first_kernel, plan_z(count), count),
+        functools.partial(first_kernel, plan_z()),
         "first",
         pos,
         [*pieces, own, peer],
         [((n, 1536), t) for n, t in heights],
-        [pltpu.VMEM((tokens, 768), F32)],
-        4 * tokens * 1536 * 1536,
+        [pltpu.VMEM((512, 768), F32)],
+        4 * 512 * 1536 * 1536,
     )
 
 
-def second_kernel(count, pos, *refs):
+def second_kernel(pos, *refs):
     pieces, refs = refs[: len(FROM_X)], refs[len(FROM_X) :]
-    own_ref, peer_ref, rows, rows_peer = refs[:4]
-    outs = refs[4:-1]
-    held = refs[-1]
-    two = 2 * count
-    wide = held.shape[1]
+    in_other, own_ref, peer_ref, rows, pack = refs[:5]
+    outs = refs[5:-2]
+    rows_peer, held = refs[-2:]
     for ref, (off, y) in zip(pieces, FROM_X):
-        at = pl.ds(place_x(pos, off, y, two), two)
-        rows[at, :] = ref[:, 0:768]
-        rows_peer[at, :] = ref[:, 768:1536]
-
-    for step in range(1536 // wide):
-        where = slice(step * wide, step * wide + wide)
+        for k, place in enumerate(place_x(pos, off, y)):
+            at = slice(k * 32, k * 32 + 32)
+            rows[place, :] = ref[at, 0:768]
+            rows_peer[place, :] = ref[at, 768:1536]
+    pack[0:256, :] = in_other[...]
+    pack[256:512, 0:768] = rows_peer[0:256, :]
+    pack[256:512, 768:1536] = rows_peer[256:512, :]
+
+    for step in range(2):
+        where = slice(step * 768, step * 768 + 768)
         out = lax.dot_general(rows[...], own_ref[768:1536, where], NT, preferred_element_type=F32)
-        out += lax.dot_general(rows_peer[...], peer_ref[768:1536, where], NT, preferred_element_type=F32)
+        out += lax.dot_general(
+            rows_peer[...], peer_ref[768:1536, where], NT, preferred_element_type=F32
+        )
         held[...] = out
 
-        def block(off, half):
-            return held[pl.ds(place_z(pos, off, half, count), count), :]
+        def put(ref, at, off, half):
+            ref[at : at + 32, where] = held[place_z(pos, off, half), :].astype(ref.dtype)
 
         up, down, keep = outs[0:4], outs[4:8], outs[8]
         for s in range(4):
-            kind = BF if s == 0 else F32
-            up[s][0:count, where] = block(4 - s, 0).astype(kind)
-            down[s][0:count, where] = block(s - 4, 1).astype(kind)
+            put(up[s], 0, 4 - s, 0)
+            put(down[s], 0, s - 4, 1)
             if s < 3:
-                up[s][count:two, where] = block(3 - s, 1).astype(kind)
-                down[s][count:two, where] = block(s - 3, 0).astype(kind)
-        keep[0:count, where] = block(0, 0)
-        keep[count:two, where] = block(0, 1)
-
-
-def second(pos, pieces, own, peer, count):
-    tokens, two = 16 * count, 2 * count
-    ring = [(two, BF), (two, F32), (two, F32), (count, F32)]
-    shapes = [((tokens, 768), BF)] * 2
-    shapes += [((n, 1536), t) for n, t in ring + ring + [(two, F32)]]
+                put(up[s], 32, 3 - s, 1)
+                put(down[s], 32, s - 3, 0)
+        put(keep, 0, 0, 0)
+        put(keep, 32, 0, 1)
+
+
+def second(pos, pieces, in_other, own, peer):
+    ring = [(64, BF), (64, F32), (64, F32), (32, F32)]
+    shapes = [((512, 768), BF), ((512, 1536), BF)]
+    shapes += [((n, 1536), t) for n, t in ring + ring + [(64, F32)]]
     return call(
-        functools.partial(second_kernel, count),
+        second_kernel,
         "second",
         pos,
-        [*pieces, own, peer],
+        [*pieces, in_other, own, peer],
         shapes,
-        [pltpu.VMEM((tokens, 768), F32)],
-        4 * tokens * 1536 * 1536,
+        [pltpu.VMEM((512, 768), BF), pltpu.VMEM((512, 768), F32)],
+        4 * 512 * 1536 * 1536,
     )
 
 
@@ -247,7 +248,9 @@
             held[owner] = ref[first : first + 128, :].reshape(2, 2, 32, -1)
     total = None
     for k, part in enumerate((own, peer)):
-        left = held[:, :, lax.rem(pos[4] + k, 2)].reshape(512, -1)
+        core = lax.rem(pos[4] + k, 2)
+        halves = [held[:, lax.rem(pos[3] + y, 2), core].reshape(256, -1) for y in range(2)]
+        left = jnp.concatenate(halves)
         term = lax.dot_general(left, part[0:512, :], TN, preferred_element_type=F32)
         total = term if total is None else total + term
     store_kept(total, mask, pl.program_id(0) * (out.shape[0] // 128), out)
@@ -272,30 +275,31 @@
     )(pos, mask, *pieces, own, peer)
 
 
-def win_kernel(mask, left0, left1, own, peer, out):
-    total = None
-    for left, right in ((left0, own), (left1, peer)):
-        term = lax.dot_general(left[...], right[...], TN, preferred_element_type=F32)
-        total = term if total is None else total + term
+def win_kernel(mask, in0, in1, peer0, peer1, acts, peer, out):
+    left = jnp.concatenate([in0[...], in1[...]])
+    total = lax.dot_general(left, acts[...], TN, preferred_element_type=F32)
+    left = jnp.concatenate([peer0[...], peer1[...]])
+    right = jnp.concatenate([peer[256:512, 0:768], peer[256:512, 768:1536]])
+    total += lax.dot_general(left, right, TN, preferred_element_type=F32)
     store_kept(total, mask, pl.program_id(0) * (out.shape[0] // 128), out)
 
 
-def win_grad(own_rows, peer_rows, own, peer, mask):
+def win_grad(rows, pack, rows_peer, pack_peer, acts, mask):
     block = 768
-    rows = pl.BlockSpec((512, block), lambda i, _: (1, i))
+    at = lambda k: pl.BlockSpec((256, block), lambda i, _: (k, i))
     return pl.pallas_call(
         win_kernel,
         grid_spec=pltpu.PrefetchScalarGridSpec(
             num_scalar_prefetch=1,
             grid=(1536 // block,),
-            in_specs=[rows, rows] + in_vmem(2),
+            in_specs=[at(2), at(0), at(2), at(0)] + in_vmem(2),
             out_specs=pl.BlockSpec((block, 768), lambda i, _: (i, 0)),
         ),
         out_shape=jax.ShapeDtypeStruct((1536, 768), BF),
         compiler_params=params(VMEM),
         cost_estimate=cost(4 * 1024 * 1536 * 768, 8 * MIB),
         name="win_grad",
-    )(mask, own_rows, peer_rows, own, peer)
+    )(mask, rows, pack, rows_peer, pack_peer, acts, pack_peer)
 
 
 def slope(values):
@@ -312,12 +316,12 @@
     f = lambda v: v.astype(F32)
     count, two = 32, 64
 
-    others = [shift(v, "ylo", 1) for v in (grad_out, inputs)]
+    other = shift(grad_out, "ylo", 1)
     shapes = [((128, 768), BF), ((64, 768), F32), ((64, 768), BF)]
     hidden, slopes, theirs = call(values_kernel, "values", pos, [pre_act], shapes, [], MIB)
     hidden_other = shift(hidden, "yhi", 1)
-    *others, hidden, theirs = together(*others, hidden, theirs)
-    sent = jnp.concatenate([grad_out, others[0], inputs, others[1]])
+    other, hidden, theirs = together(other, hidden, theirs)
+    sent = jnp.concatenate([grad_out, other, inputs])
     up1, down1 = both_ways("z", sent, sent)
     own = masked(after(mask_out, sent), mask_in, w_out, w_in, theirs)
     up1, down1, own, hidden_other = together(up1, down1, own, hidden_other)
@@ -328,18 +332,19 @@
     up2, down2 = together(up2, down2)
     up3, down3 = both_ways("z", up2, down2)
     up3, down3, hid_up, hid_down = together(up3, down3, hid_up, hid_down)
-    up4, down4 = both_ways("z", up3[: 2 * count], down3[2 * count :])
+    up4, down4 = both_ways("z", up3[:64], down3[64:])
     hid_far = shift(after(hid_up, up3), "x", 1)
     up4, down4, hid_far = together(up4, down4, hid_far)
     pieces = [sent, up1, down1, up2, down2, up3, down3, up4, down4]
 
-    rows, far1, down1, up1, far0, up0, down0, keep0, keep1 = first(pos, pieces, own, peer, count)
+    rows, ins, far1, down1, up1, far0, up0, down0, keep0, keep1 = first(pos, pieces, own, peer)
     got, down1 = both_ways("x", far1, down1)
+    in_other = shift(ins, "ylo", 1)
     slopes = jnp.concatenate([slopes, slope(after(peer, keep1)[1536:, :768])], axis=1)
     rows_peer = shift(after(rows, slopes), "core", 1)
     got, down1, slopes = together(got, down1, slopes)
     up1, got = both_ways("x", (up1 + f(got)).astype(BF), far0)
-    up1, got = together(up1, got)
+    up1, got, in_other = together(up1, got, in_other)
     other = shift((keep1 + f(down1) + f(up1)).astype(BF), "yhi", 1)
     up0, down0 = both_ways("x", up0, (down0 + f(got)).astype(BF))
     act = ((keep0 + f(up0) + f(down0) + f(other)) * slopes).astype(BF)
@@ -354,17 +359,17 @@
     far1 = shift(down1, "x", -1)
 
     acts = [act, other, up0, down0, up1, down1, far0, far1]
-    outs = second(pos, acts, own, peer, count)
-    acts_own, acts_peer = outs[0:2]
+    outs = second(pos, acts, in_other, own, peer)
+    acts, pack = outs[0:2]
     up, down, keep = outs[2:6], outs[6:10], outs[10]
     send_up, send_down = up[0], down[0]
     for s in range(1, 4):
         got_up, got_down = shift(send_up, "z", 1), shift(send_down, "z", -1)
         if s == 1:
-            acts_peer = shift(acts_peer, "core", 1)
+            pack_peer = shift(pack, "core", 1)
         elif s == 2:
             grad_w_in = win_grad(
-                rows, rows_peer, acts_own, after(acts_peer, send_up, send_down), mask_in
+                rows, pack, rows_peer, after(pack_peer, send_up, send_down), acts, mask_in
             )
             got_up, got_down, _ = lax.optimization_barrier((got_up, got_down, grad_w_in))
         n = two if s < 3 else count

time: 155 us -> 149 us (0.961)
  starting transfers between devices: 55.6 us -> 51.8 us
  waiting for transfers between devices: 69.3 us -> 67.5 us
    ppermute x40, starting transfers between devices: 55.6 us -> 51.8 us  [shift(): lax.ppermute(value, axis, [(i, (i + by) % count) for i in range(count)])]
    ppermute x40, waiting for transfers between devices: 69.3 us -> 67.5 us  [shift(): lax.ppermute(value, axis, [(i, (i + by) % count) for i in range(count)])]
    unnamed x15 -> x14, local copies, waits for them, and re-layouts: 7.58 us -> 6.67 us
  transfers between devices with their start and end apart: 40 -> 40, of which waited for: 19 -> 23; matrix products, arithmetic and copies ran while one was open for 1% -> 2% of each run, Pallas kernels for 8% -> 8%
where the time goes in v1:
time: 149 us
  waiting for transfers between devices  67.5 us (45%)
  starting transfers between devices  51.8 us (35%)
  Pallas kernels  19.6 us (13%)
  local copies, waits for them, and re-layouts  7.7 us (5%)
    ppermute x40, waiting for transfers between devices, shift(): lax.ppermute(value, axis, [(i, (i + by) % count) for i in range(count)])  67.5 us
    ppermute x40, starting transfers between devices, shift(): lax.ppermute(value, axis, [(i, (i + by) % count) for i in range(count)])  51.8 us
    pallas_call x3, Pallas kernels, call(): pl.pallas_call(kernel, in_specs=[pl.BlockSpec(memory_space=pltpu.SMEM)] +...  7.82 us
    unnamed x14, local copies, waits for them, and re-layouts  6.67 us
    pallas_call x1, Pallas kernels, wout_grad(): pl.pallas_call(functools.partial(wout_kernel, plan_x(128)), grid_spec=plt...  4.85 us
    pallas_call x1, Pallas kernels, win_grad(): pl.pallas_call(win_kernel, grid_spec=pltpu.PrefetchScalarGridSpec(num_sca...  4.79 us
  transfers between devices with their start and end apart: 40, of which 23 were waited for; matrix products, arithmetic and copies ran while one was open for 2% of the time, Pallas kernels for 8%

profile of v1, /device:TPU:6, one launch (start us, length us, event | category | flops | bytes accessed | tf_op | source)
XLA Modules:
  0.0 148.7 jit_solution(9805733866845072780)
XLA Ops:
  0.6 1.7 %collective-permute-start = (bf16[32,1536]{1,0:T(8,128)(2,1)}, bf16[32,1536]{1,0:T(8,128)(2,1)S(1)}, u32[]{:S(2)}, u32[]{:S(2)}) collective-permute-start(bf16[32,1536]{1,0:T(8,128)(2,1)} %param.8), channel_id=1, source_target_pairs={{0,2},{2,0},{1,3},{3,1},{4,6},{6,4},{5,7},{7,5},{8,10},{10,8},{9,1... | collective-permute-start | bytes 294920 | tf_op jit(solution)/shard_map/ppermute | solution.py:35
  2.3 0.9 constant_dynamic-update-slice_fusion.2
  3.3 0.9 copy-done.2
  4.2 0.8 values.1
  5.0 0.5 collective-permute-done
  5.6 0.9 constant_dynamic-update-slice_fusion.refs_0_
  6.5 5.9 %collective-permute-start.2 = (bf16[96,1536]{1,0:T(8,128)(2,1)S(1)}, bf16[96,1536]{1,0:T(8,128)(2,1)S(1)}, u32[]{:S(2)}, u32[]{:S(2)}) collective-permute-start(bf16[96,1536]{1,0:T(8,128)(2,1)S(1)} %constant_dynamic-update-slice_fusion.refs_0_), channel_id=1, source_target_pairs={{0,28},{4,0},{8,4},{12,8},{16,12},{20,16},{24,20},{28,24},{1,29},{... | collective-permute-start | bytes 884744 | tf_op jit(solution)/shard_map/ppermute | solution.py:35
  12.3 3.2 %collective-permute-start.3 = (bf16[128,768]{1,0:T(8,128)(2,1)S(1)}, bf16[128,768]{1,0:T(8,128)(2,1)S(1)}, u32[]{:S(2)}, u32[]{:S(2)}) collective-permute-start(bf16[128,768]{1,0:T(8,128)(2,1)S(1)} %get-tuple-element.70), channel_id=1, source_target_pairs={{0,128},{128,0},{1,129},{129,1},{2,130},{130,2},{3,131},{131,3},{4... | collective-permute-start | bytes 589832 | tf_op jit(solution)/shard_map/ppermute | solution.py:35
  15.5 0.8 copy.10.mask_in.mask
  16.3 1.7 %copy-done = bf16[768,1536]{1,0:T(8,128)(2,1)S(1)} copy-done((bf16[768,1536]{1,0:T(8,128)(2,1)S(1)}, bf16[768,1536]{1,0:T(8,128)(2,1)}, u32[]{:S(2)}) %copy-start) | copy-done | bytes 2359320
  18.0 1.7 %copy-done.1 = bf16[1536,768]{1,0:T(8,128)(2,1)S(1)} copy-done((bf16[1536,768]{1,0:T(8,128)(2,1)S(1)}, bf16[1536,768]{1,0:T(8,128)(2,1)}, u32[]{:S(2)}) %copy-start.1) | copy-done | bytes 2359320
  19.6 0.7 copy-done.3
  20.3 2.1 %masked.1.refs_9_ = bf16[1600,1536]{1,0:T(8,128)(2,1)S(1)} custom-call(s32[6,12]{1,0:T(8,128)S(1)} %copy-done.3, s32[12,6]{1,0:T(8,128)S(1)} %copy.10.mask_in.mask, bf16[768,1536]{1,0:T(8,128)(2,1)S(1)} %copy-done, bf16[1536,768]{1,0:T(8,128)(2,1)S(1)} %copy-done.1, bf16[64,768]{1,0:T(8,128)(2,1)S(1)} %get-tuple-element.65.theirs), custom_call_target="tpu_custom_call" | custom-call | bytes 4194304 | tf_op jit(solution)/shard_map/masked/pallas_call | solution.py:124
  22.7 3.3 %collective-permute-start.5 = (bf16[96,1536]{1,0:T(8,128)(2,1)S(1)}, bf16[96,1536]{1,0:T(8,128)(2,1)S(1)}, u32[]{:S(2)}, u32[]{:S(2)}) collective-permute-start(bf16[96,1536]{1,0:T(8,128)(2,1)S(1)} %collective-permute-done.2.refs_2_), channel_id=1, source_target_pairs={{0,28},{4,0},{8,4},{12,8},{16,12},{20,16},{24,20},{28,24},{1,29},{... | collective-permute-start | bytes 884744 | tf_op jit(solution)/shard_map/ppermute | solution.py:35
  26.0 0.9 collective-permute-start.9
  26.9 2.4 %collective-permute-start.8 = (bf16[256,768]{1,0:T(8,128)(2,1)S(1)}, bf16[256,768]{1,0:T(8,128)(2,1)S(1)}, u32[]{:S(2)}, u32[]{:S(2)}) collective-permute-start(bf16[256,768]{1,0:T(8,128)(2,1)S(1)} %constant_dynamic-update-slice_fusion.3.refs_0_), channel_id=1, source_target_pairs={{0,32},{32,64},{64,96},{96,0},{1,33},{33,65},{65,97},{97,1},{2,34}... | collective-permute-start | bytes 1179656 | tf_op jit(solution)/shard_map/ppermute | solution.py:35
  29.3 4.1 %collective-permute-done.4.refs_3_ = bf16[96,1536]{1,0:T(8,128)(2,1)S(1)} collective-permute-done((bf16[96,1536]{1,0:T(8,128)(2,1)S(1)}, bf16[96,1536]{1,0:T(8,128)(2,1)S(1)}, u32[]{:S(2)}, u32[]{:S(2)}) %collective-permute-start.4) | collective-permute-done | bytes 294944 | tf_op jit(solution)/shard_map/ppermute | solution.py:35
  33.5 3.2 %collective-permute-start.7 = (bf16[96,1536]{1,0:T(8,128)(2,1)S(1)}, bf16[96,1536]{1,0:T(8,128)(2,1)S(1)}, u32[]{:S(2)}, u32[]{:S(2)}) collective-permute-start(bf16[96,1536]{1,0:T(8,128)(2,1)S(1)} %collective-permute-done.5.refs_4_), channel_id=1, source_target_pairs={{0,28},{4,0},{8,4},{12,8},{16,12},{20,16},{24,20},{28,24},{1,29},{... | collective-permute-start | bytes 884744 | tf_op jit(solution)/shard_map/ppermute | solution.py:35
  36.7 1.7 %collective-permute-done.9.refs_2_ = bf16[256,768]{1,0:T(8,128)(2,1)S(1)} collective-permute-done((bf16[256,768]{1,0:T(8,128)(2,1)S(1)}, bf16[256,768]{1,0:T(8,128)(2,1)S(1)}, u32[]{:S(2)}, u32[]{:S(2)}) %collective-permute-start.9) | collective-permute-done | bytes 393248 | tf_op jit(solution)/shard_map/ppermute | solution.py:35
  38.4 5.1 %collective-permute-done.6.refs_5_ = bf16[96,1536]{1,0:T(8,128)(2,1)S(1)} collective-permute-done((bf16[96,1536]{1,0:T(8,128)(2,1)S(1)}, bf16[96,1536]{1,0:T(8,128)(2,1)S(1)}, u32[]{:S(2)}, u32[]{:S(2)}) %collective-permute-start.6) | collective-permute-done | bytes 294944 | tf_op jit(solution)/shard_map/ppermute | solution.py:35
  43.5 0.5 collective-permute-start.12
  44.0 0.8 collective-permute-start.10
  44.8 2.7 %collective-permute-start.11 = (bf16[32,1536]{1,0:T(8,128)(2,1)S(1)}, bf16[32,1536]{1,0:T(8,128)(2,1)S(1)}, u32[]{:S(2)}, u32[]{:S(2)}) collective-permute-start(bf16[32,1536]{1,0:T(8,128)(2,1)S(1)} %slice.28), channel_id=1, source_target_pairs={{0,28},{4,0},{8,4},{12,8},{16,12},{20,16},{24,20},{28,24},{1,29},{... | collective-permute-start | bytes 294920 | tf_op jit(solution)/shard_map/ppermute | solution.py:35
  47.5 2.2 %collective-permute-done.11.refs_8_ = bf16[32,1536]{1,0:T(8,128)(2,1)S(1)} collective-permute-done((bf16[32,1536]{1,0:T(8,128)(2,1)S(1)}, bf16[32,1536]{1,0:T(8,128)(2,1)S(1)}, u32[]{:S(2)}, u32[]{:S(2)}) %collective-permute-start.11) | collective-permute-done | bytes 98336 | tf_op jit(solution)/shard_map/ppermute | solution.py:35
  49.7 1.2 collective-permute-done.10.refs_7_
  50.9 2.5 %collective-permute-done.12.refs_3_ = bf16[256,768]{1,0:T(8,128)(2,1)S(1)} collective-permute-done((bf16[256,768]{1,0:T(8,128)(2,1)S(1)}, bf16[256,768]{1,0:T(8,128)(2,1)S(1)}, u32[]{:S(2)}, u32[]{:S(2)}) %collective-permute-start.12) | collective-permute-done | bytes 393248 | tf_op jit(solution)/shard_map/ppermute | solution.py:35
  53.4 3.5 %first.1 = (bf16[768,1536]{1,0:T(8,128)(2,1)S(1)}, bf16[256,1536]{1,0:T(8,128)(2,1)S(1)}, bf16[64,1536]{1,0:T(8,128)(2,1)S(1)}, bf16[64,1536]{1,0:T(8,128)(2,1)S...) custom-call(s32[5]{0:T(128)S(1)} %stack.23.pos, ...), custom_call_target="tpu_custom_call" | custom-call | flops 4831838208 | bytes 1048576 | tf_op jit(solution)/shard_map/first/pallas_call | solution.py:90
  57.1 1.8 %collective-permute-start.15 = (bf16[64,1536]{1,0:T(8,128)(2,1)S(1)}, bf16[64,1536]{1,0:T(8,128)(2,1)S(1)}, u32[]{:S(2)}, u32[]{:S(2)}) collective-permute-start(bf16[64,1536]{1,0:T(8,128)(2,1)S(1)} %get-tuple-element.83), channel_id=1, source_target_pairs={{0,32},{32,64},{64,96},{96,0},{1,33},{33,65},{65,97},{97,1},{2,34}... | collective-permute-start | bytes 589832 | tf_op jit(solution)/shard_map/ppermute | solution.py:35
  58.9 0.3 collective-permute-start.16
  59.2 0.7 collective-permute-start.19
  60.1 0.9 collective-permute-start.18
  60.9 1.9 %collective-permute-done.15 = bf16[64,1536]{1,0:T(8,128)(2,1)S(1)} collective-permute-done((bf16[64,1536]{1,0:T(8,128)(2,1)S(1)}, bf16[64,1536]{1,0:T(8,128)(2,1)S(1)}, u32[]{:S(2)}, u32[]{:S(2)}) %collective-permute-start.15) | collective-permute-done | bytes 196640 | tf_op jit(solution)/shard_map/ppermute | solution.py:35
  62.9 4.3 %collective-permute-done.16 = bf16[64,1536]{1,0:T(8,128)(2,1)S(1)} collective-permute-done((bf16[64,1536]{1,0:T(8,128)(2,1)S(1)}, bf16[64,1536]{1,0:T(8,128)(2,1)S(1)}, u32[]{:S(2)}, u32[]{:S(2)}) %collective-permute-start.16) | collective-permute-done | bytes 196640 | tf_op jit(solution)/shard_map/ppermute | solution.py:35
  67.4 0.3 collective-permute-start.14
  67.7 2.3 %collective-permute-done.18 = bf16[64,1536]{1,0:T(8,128)(2,1)S(1)} collective-permute-done((bf16[64,1536]{1,0:T(8,128)(2,1)S(1)}, bf16[64,1536]{1,0:T(8,128)(2,1)S(1)}, u32[]{:S(2)}, u32[]{:S(2)}) %collective-permute-start.18) | collective-permute-done | bytes 196640 | tf_op jit(solution)/shard_map/ppermute | solution.py:35
  70.0 3.0 %collective-permute-done.17 = bf16[64,1536]{1,0:T(8,128)(2,1)S(1)} collective-permute-done((bf16[64,1536]{1,0:T(8,128)(2,1)S(1)}, bf16[64,1536]{1,0:T(8,128)(2,1)S(1)}, u32[]{:S(2)}, u32[]{:S(2)}) %collective-permute-start.17) | collective-permute-done | bytes 196640 | tf_op jit(solution)/shard_map/ppermute | solution.py:35
  73.0 3.5 %collective-permute-done.19.refs_8_ = bf16[256,1536]{1,0:T(8,128)(2,1)S(1)} collective-permute-done((bf16[256,1536]{1,0:T(8,128)(2,1)S(1)}, bf16[256,1536]{1,0:T(8,128)(2,1)S(1)}, u32[]{:S(2)}, u32[]{:S(2)}) %collective-permute-start.19) | collective-permute-done | bytes 786464 | tf_op jit(solution)/shard_map/ppermute | solution.py:35
  76.6 1.0 collective-permute-start.20
  77.7 0.5 collective-permute-start.21
  78.2 5.5 %collective-permute-done.20 = bf16[64,1536]{1,0:T(8,128)(2,1)S(1)} collective-permute-done((bf16[64,1536]{1,0:T(8,128)(2,1)S(1)}, bf16[64,1536]{1,0:T(8,128)(2,1)S(1)}, u32[]{:S(2)}, u32[]{:S(2)}) %collective-permute-start.20) | collective-permute-done | bytes 196640 | tf_op jit(solution)/shard_map/ppermute | solution.py:35
  83.7 1.2 collective-permute-done.21
  85.0 0.2 collective-permute-start.24
  85.3 3.1 %collective-permute-start.23 = (bf16[64,1536]{1,0:T(8,128)(2,1)S(1)}, bf16[64,1536]{1,0:T(8,128)(2,1)S(1)}, u32[]{:S(2)}, u32[]{:S(2)}) collective-permute-start(bf16[64,1536]{1,0:T(8,128)(2,1)S(1)} %multiply_convert_fusion.refs_0_), channel_id=1, source_target_pairs={{0,32},{32,64},{64,96},{96,0},{1,33},{33,65},{65,97},{97,1},{2,34}... | collective-permute-start | bytes 589832 | tf_op jit(solution)/shard_map/ppermute | solution.py:35
  88.4 0.4 collective-permute-start.22
  88.8 4.8 %wout_grad.1 = bf16[768,1536]{1,0:T(8,128)(2,1)} custom-call(s32[5]{0:T(128)S(1)} %stack.23.pos, s32[6,12]{1,0:T(8,128)S(1)} %copy-done.4, bf16[256,768]{1,0:T(8,128)(2,1)S(1)} %constant_dynamic-update-slice_fusion.3.refs_0_, bf16[256,768]{1,0:T(8,128)(2,1)S(1)} %collective-permute-done.8.refs_1_, bf16[256,768]{1,0:T(8,128)(2,1)S(1)} %collective-permute-done.9.refs_2_, ...), custom_call_target="tpu_custom_call" | custom-call | flops 4831838208 | bytes 8388608 | tf_op jit(solution)/shard_map/wout_grad/pallas_call | solution.py:261
  93.7 0.3 collective-permute-done.23.refs_2_
  94.0 1.6 %collective-permute-done.22.refs_1_ = bf16[64,1536]{1,0:T(8,128)(2,1)S(1)} collective-permute-done((bf16[64,1536]{1,0:T(8,128)(2,1)S(1)}, bf16[64,1536]{1,0:T(8,128)(2,1)S(1)}, u32[]{:S(2)}, u32[]{:S(2)}) %collective-permute-start.22) | collective-permute-done | bytes 196640 | tf_op jit(solution)/shard_map/ppermute | solution.py:35
  95.5 0.8 collective-permute-start.27
  96.3 2.5 %collective-permute-start.26 = (bf16[64,1536]{1,0:T(8,128)(2,1)S(1)}, bf16[64,1536]{1,0:T(8,128)(2,1)S(1)}, u32[]{:S(2)}, u32[]{:S(2)}) collective-permute-start(bf16[64,1536]{1,0:T(8,128)(2,1)S(1)} %collective-permute-done.22.refs_1_), channel_id=1, source_target_pairs={{0,32},{32,64},{64,96},{96,0},{1,33},{33,65},{65,97},{97,1},{2,34}... | collective-permute-start | bytes 589832 | tf_op jit(solution)/shard_map/ppermute | solution.py:35
  98.9 3.6 %collective-permute-done.27.refs_5_ = bf16[64,1536]{1,0:T(8,128)(2,1)S(1)} collective-permute-done((bf16[64,1536]{1,0:T(8,128)(2,1)S(1)}, bf16[64,1536]{1,0:T(8,128)(2,1)S(1)}, u32[]{:S(2)}, u32[]{:S(2)}) %collective-permute-start.27) | collective-permute-done | bytes 196640 | tf_op jit(solution)/shard_map/ppermute | solution.py:35
  102.5 1.9 %collective-permute-done.28.refs_6_ = bf16[64,1536]{1,0:T(8,128)(2,1)S(1)} collective-permute-done((bf16[64,1536]{1,0:T(8,128)(2,1)S(1)}, bf16[64,1536]{1,0:T(8,128)(2,1)S(1)}, u32[]{:S(2)}, u32[]{:S(2)}) %collective-permute-start.28) | collective-permute-done | bytes 196640 | tf_op jit(solution)/shard_map/ppermute | solution.py:35
  104.4 5.0 %collective-permute-done.29.refs_7_ = bf16[64,1536]{1,0:T(8,128)(2,1)S(1)} collective-permute-done((bf16[64,1536]{1,0:T(8,128)(2,1)S(1)}, bf16[64,1536]{1,0:T(8,128)(2,1)S(1)}, u32[]{:S(2)}, u32[]{:S(2)}) %collective-permute-start.29) | collective-permute-done | bytes 196640 | tf_op jit(solution)/shard_map/ppermute | solution.py:35
  109.4 3.5 %second.1 = (bf16[512,768]{1,0:T(8,128)(2,1)S(1)}, bf16[512,1536]{1,0:T(8,128)(2,1)S(1)}, bf16[64,1536]{1,0:T(8,128)(2,1)S(1)}, f32[64,1536]{1,0:T(8,128)S(1)}, ...) custom-call(s32[5]{0:T(128)S(1)} %stack.23.pos, ...), custom_call_target="tpu_custom_call" | custom-call | flops 4831838208 | bytes 1048576 | tf_op jit(solution)/shard_map/second/pallas_call | solution.py:90
  113.1 3.2 %collective-permute-start.32 = (bf16[64,1536]{1,0:T(8,128)(2,1)S(1)}, bf16[64,1536]{1,0:T(8,128)(2,1)S(1)}, u32[]{:S(2)}, u32[]{:S(2)}) collective-permute-start(bf16[64,1536]{1,0:T(8,128)(2,1)S(1)} %get-tuple-element.109), channel_id=1, source_target_pairs={{0,28},{4,0},{8,4},{12,8},{16,12},{20,16},{24,20},{28,24},{1,29},{... | collective-permute-start | bytes 589832 | tf_op jit(solution)/shard_map/ppermute | solution.py:35
  116.3 5.2 %collective-permute-done.30 = bf16[64,1536]{1,0:T(8,128)(2,1)S(1)} collective-permute-done((bf16[64,1536]{1,0:T(8,128)(2,1)S(1)}, bf16[64,1536]{1,0:T(8,128)(2,1)S(1)}, u32[]{:S(2)}, u32[]{:S(2)}) %collective-permute-start.30) | collective-permute-done | bytes 196640 | tf_op jit(solution)/shard_map/ppermute | solution.py:35
  121.7 3.3 %collective-permute-start.33 = (bf16[64,1536]{1,0:T(8,128)(2,1)S(1)}, bf16[64,1536]{1,0:T(8,128)(2,1)S(1)}, u32[]{:S(2)}, u32[]{:S(2)}) collective-permute-start(bf16[64,1536]{1,0:T(8,128)(2,1)S(1)} %add_convert_fusion.2), channel_id=1, source_target_pairs={{0,28},{4,0},{8,4},{12,8},{16,12},{20,16},{24,20},{28,24},{1,29},{... | collective-permute-start | bytes 589832 | tf_op jit(solution)/shard_map/ppermute | solution.py:35
  125.0 4.8 %win_grad.1 = bf16[1536,768]{1,0:T(8,128)(2,1)} custom-call(s32[12,6]{1,0:T(8,128)S(1)} %copy.10.mask_in.mask, bf16[768,1536]{1,0:T(8,128)(2,1)S(1)} %get-tuple-element.98.refs_4_.in0, bf16[512,1536]{1,0:T(8,128)(2,1)S(1)} %get-tuple-element.110.in1, bf16[768,1536]{1,0:T(8,128)(2,1)S(1)} %collective-permute-done.25.refs_5_.peer0, ...), custom_call_target="tpu_custom_call" | custom-call | flops 4831838208 | bytes 8388608 | tf_op jit(solution)/shard_map/win_grad/pallas_call | solution.py:290
  129.8 2.7 %collective-permute-start.35 = (bf16[64,1536]{1,0:T(8,128)(2,1)S(1)}, bf16[64,1536]{1,0:T(8,128)(2,1)S(1)}, u32[]{:S(2)}, u32[]{:S(2)}) collective-permute-start(bf16[64,1536]{1,0:T(8,128)(2,1)S(1)} %add_convert_fusion.1), channel_id=1, source_target_pairs={{0,28},{4,0},{8,4},{12,8},{16,12},{20,16},{24,20},{28,24},{1,29},{... | collective-permute-start | bytes 589832 | tf_op jit(solution)/shard_map/ppermute | solution.py:35
  132.6 3.2 %collective-permute-done.35 = bf16[64,1536]{1,0:T(8,128)(2,1)S(1)} collective-permute-done((bf16[64,1536]{1,0:T(8,128)(2,1)S(1)}, bf16[64,1536]{1,0:T(8,128)(2,1)S(1)}, u32[]{:S(2)}, u32[]{:S(2)}) %collective-permute-start.35) | collective-permute-done | bytes 196640 | tf_op jit(solution)/shard_map/ppermute | solution.py:35
  135.8 3.6 %collective-permute-start.38 = (bf16[32,1536]{1,0:T(8,128)(2,1)S(1)}, bf16[32,1536]{1,0:T(8,128)(2,1)S(1)}, u32[]{:S(2)}, u32[]{:S(2)}) collective-permute-start(bf16[32,1536]{1,0:T(8,128)(2,1)S(1)} %add_convert_fusion.9), channel_id=1, source_target_pairs={{0,28},{4,0},{8,4},{12,8},{16,12},{20,16},{24,20},{28,24},{1,29},{... | collective-permute-start | bytes 294920 | tf_op jit(solution)/shard_map/ppermute | solution.py:35
  139.5 2.2 %collective-permute-done.38 = bf16[32,1536]{1,0:T(8,128)(2,1)S(1)} collective-permute-done((bf16[32,1536]{1,0:T(8,128)(2,1)S(1)}, bf16[32,1536]{1,0:T(8,128)(2,1)S(1)}, u32[]{:S(2)}, u32[]{:S(2)}) %collective-permute-start.38) | collective-permute-done | bytes 98336 | tf_op jit(solution)/shard_map/ppermute | solution.py:35
  141.8 0.9 collective-permute-start.39
  142.7 5.3 %collective-permute-done.37 = bf16[32,1536]{1,0:T(8,128)(2,1)S(1)} collective-permute-done((bf16[32,1536]{1,0:T(8,128)(2,1)S(1)}, bf16[32,1536]{1,0:T(8,128)(2,1)S(1)}, u32[]{:S(2)}, u32[]{:S(2)}) %collective-permute-start.37) | collective-permute-done | bytes 98336 | tf_op jit(solution)/shard_map/ppermute | solution.py:35
  148.0 0.7 add_convert_fusion.7
  (54 shorter events, 1.7 us)
Async XLA Ops:
  0.6 4.9 %collective-permute-start = (bf16[32,1536]{1,0:T(8,128)(2,1)}, bf16[32,1536]{1,0:T(8,128)(2,1)S(1)}, u32[]{:S(2)}, u32[]{:S(2)}) collective-permute-start(bf16[32,1536]{1,0:T(8,128)(2,1)} %param.8), channel_id=1, source_target_pairs={{0,2},{2,0},{1,3},{3,1},{4,6},{6,4},{5,7},{7,5},{8,10},{10,8},{9,1... | collective-permute-start | bytes 294920 | tf_op jit(solution)/shard_map/ppermute | solution.py:35
  3.3 0.9 copy-start.2
  6.5 16.0 %collective-permute-start.2 = (bf16[96,1536]{1,0:T(8,128)(2,1)S(1)}, bf16[96,1536]{1,0:T(8,128)(2,1)S(1)}, u32[]{:S(2)}, u32[]{:S(2)}) collective-permute-start(bf16[96,1536]{1,0:T(8,128)(2,1)S(1)} %constant_dynamic-update-slice_fusion.refs_0_), channel_id=1, source_target_pairs={{0,28},{4,0},{8,4},{12,8},{16,12},{20,16},{24,20},{28,24},{1,29},{... | collective-permute-start | bytes 884744 | tf_op jit(solution)/shard_map/ppermute | solution.py:35
  12.3 10.2 %collective-permute-start.1 = (bf16[96,1536]{1,0:T(8,128)(2,1)S(1)}, bf16[96,1536]{1,0:T(8,128)(2,1)S(1)}, u32[]{:S(2)}, u32[]{:S(2)}) collective-permute-start(bf16[96,1536]{1,0:T(8,128)(2,1)S(1)} %constant_dynamic-update-slice_fusion.refs_0_), channel_id=1, source_target_pairs={{0,4},{4,8},{8,12},{12,16},{16,20},{20,24},{24,28},{28,0},{1,5},{5... | collective-permute-start | bytes 884744 | tf_op jit(solution)/shard_map/ppermute | solution.py:35
  12.3 10.1 %collective-permute-start.3 = (bf16[128,768]{1,0:T(8,128)(2,1)S(1)}, bf16[128,768]{1,0:T(8,128)(2,1)S(1)}, u32[]{:S(2)}, u32[]{:S(2)}) collective-permute-start(bf16[128,768]{1,0:T(8,128)(2,1)S(1)} %get-tuple-element.70), channel_id=1, source_target_pairs={{0,128},{128,0},{1,129},{129,1},{2,130},{130,2},{3,131},{131,3},{4... | collective-permute-start | bytes 589832 | tf_op jit(solution)/shard_map/ppermute | solution.py:35
  16.3 1.7 %copy-start = (bf16[768,1536]{1,0:T(8,128)(2,1)S(1)}, bf16[768,1536]{1,0:T(8,128)(2,1)}, u32[]{:S(2)}) copy-start(bf16[768,1536]{1,0:T(8,128)(2,1)} %w_out.1) | copy-start | bytes 7077892
  18.0 1.7 %copy-start.1 = (bf16[1536,768]{1,0:T(8,128)(2,1)S(1)}, bf16[1536,768]{1,0:T(8,128)(2,1)}, u32[]{:S(2)}) copy-start(bf16[1536,768]{1,0:T(8,128)(2,1)} %w_in.1) | copy-start | bytes 7077892
  19.6 0.7 copy-start.3
  22.5 31.0 %collective-permute-start.13 = (bf16[1600,1536]{1,0:T(8,128)(2,1)S(1)}, bf16[1600,1536]{1,0:T(8,128)(2,1)S(1)}, u32[]{:S(2)}, u32[]{:S(2)}) collective-permute-start(bf16[1600,1536]{1,0:T(8,128)(2,1)S(1)} %masked.1.refs_9_), channel_id=1, source_target_pairs={{0,1},{1,0},{2,3},{3,2},{4,5},{5,4},{6,7},{7,6},{8,9},{9,8},{10,11... | collective-permute-start | bytes 14745608 | tf_op jit(solution)/shard_map/ppermute | solution.py:35
  22.6 10.9 %collective-permute-start.4 = (bf16[96,1536]{1,0:T(8,128)(2,1)S(1)}, bf16[96,1536]{1,0:T(8,128)(2,1)S(1)}, u32[]{:S(2)}, u32[]{:S(2)}) collective-permute-start(bf16[96,1536]{1,0:T(8,128)(2,1)S(1)} %collective-permute-done.1.refs_1_), channel_id=1, source_target_pairs={{0,4},{4,8},{8,12},{12,16},{16,20},{20,24},{24,28},{28,0},{1,5},{5... | collective-permute-start | bytes 884744 | tf_op jit(solution)/shard_map/ppermute | solution.py:35
  22.7 10.8 %collective-permute-start.5 = (bf16[96,1536]{1,0:T(8,128)(2,1)S(1)}, bf16[96,1536]{1,0:T(8,128)(2,1)S(1)}, u32[]{:S(2)}, u32[]{:S(2)}) collective-permute-start(bf16[96,1536]{1,0:T(8,128)(2,1)S(1)} %collective-permute-done.2.refs_2_), channel_id=1, source_target_pairs={{0,28},{4,0},{8,4},{12,8},{16,12},{20,16},{24,20},{28,24},{1,29},{... | collective-permute-start | bytes 884744 | tf_op jit(solution)/shard_map/ppermute | solution.py:35
  26.0 12.4 %collective-permute-start.9 = (bf16[256,768]{1,0:T(8,128)(2,1)S(1)}, bf16[256,768]{1,0:T(8,128)(2,1)S(1)}, u32[]{:S(2)}, u32[]{:S(2)}) collective-permute-start(bf16[256,768]{1,0:T(8,128)(2,1)S(1)} %constant_dynamic-update-slice_fusion.3.refs_0_), channel_id=1, source_target_pairs={{0,96},{32,0},{64,32},{96,64},{1,97},{33,1},{65,33},{97,65},{2,98}... | collective-permute-start | bytes 1179656 | tf_op jit(solution)/shard_map/ppermute | solution.py:35
  26.9 11.5 %collective-permute-start.8 = (bf16[256,768]{1,0:T(8,128)(2,1)S(1)}, bf16[256,768]{1,0:T(8,128)(2,1)S(1)}, u32[]{:S(2)}, u32[]{:S(2)}) collective-permute-start(bf16[256,768]{1,0:T(8,128)(2,1)S(1)} %constant_dynamic-update-slice_fusion.3.refs_0_), channel_id=1, source_target_pairs={{0,32},{32,64},{64,96},{96,0},{1,33},{33,65},{65,97},{97,1},{2,34}... | collective-permute-start | bytes 1179656 | tf_op jit(solution)/shard_map/ppermute | solution.py:35
  33.5 10.0 %collective-permute-start.6 = (bf16[96,1536]{1,0:T(8,128)(2,1)S(1)}, bf16[96,1536]{1,0:T(8,128)(2,1)S(1)}, u32[]{:S(2)}, u32[]{:S(2)}) collective-permute-start(bf16[96,1536]{1,0:T(8,128)(2,1)S(1)} %collective-permute-done.4.refs_3_), channel_id=1, source_target_pairs={{0,4},{4,8},{8,12},{12,16},{16,20},{20,24},{24,28},{28,0},{1,5},{5... | collective-permute-start | bytes 884744 | tf_op jit(solution)/shard_map/ppermute | solution.py:35
  33.5 10.0 %collective-permute-start.7 = (bf16[96,1536]{1,0:T(8,128)(2,1)S(1)}, bf16[96,1536]{1,0:T(8,128)(2,1)S(1)}, u32[]{:S(2)}, u32[]{:S(2)}) collective-permute-start(bf16[96,1536]{1,0:T(8,128)(2,1)S(1)} %collective-permute-done.5.refs_4_), channel_id=1, source_target_pairs={{0,28},{4,0},{8,4},{12,8},{16,12},{20,16},{24,20},{28,24},{1,29},{... | collective-permute-start | bytes 884744 | tf_op jit(solution)/shard_map/ppermute | solution.py:35
  43.5 10.0 %collective-permute-start.12 = (bf16[256,768]{1,0:T(8,128)(2,1)S(1)}, bf16[256,768]{1,0:T(8,128)(2,1)S(1)}, u32[]{:S(2)}, u32[]{:S(2)}) collective-permute-start(bf16[256,768]{1,0:T(8,128)(2,1)S(1)} %collective-permute-done.8.refs_1_), channel_id=1, source_target_pairs={{0,32},{32,64},{64,96},{96,0},{1,33},{33,65},{65,97},{97,1},{2,34}... | collective-permute-start | bytes 1179656 | tf_op jit(solution)/shard_map/ppermute | solution.py:35
  44.0 7.0 %collective-permute-start.10 = (bf16[64,1536]{1,0:T(8,128)(2,1)S(1)}, bf16[64,1536]{1,0:T(8,128)(2,1)S(1)}, u32[]{:S(2)}, u32[]{:S(2)}) collective-permute-start(bf16[64,1536]{1,0:T(8,128)(2,1)S(1)} %slice.27), channel_id=1, source_target_pairs={{0,4},{4,8},{8,12},{12,16},{16,20},{20,24},{24,28},{28,0},{1,5},{5... | collective-permute-start | bytes 589832 | tf_op jit(solution)/shard_map/ppermute | solution.py:35
  44.8 5.0 %collective-permute-start.11 = (bf16[32,1536]{1,0:T(8,128)(2,1)S(1)}, bf16[32,1536]{1,0:T(8,128)(2,1)S(1)}, u32[]{:S(2)}, u32[]{:S(2)}) collective-permute-start(bf16[32,1536]{1,0:T(8,128)(2,1)S(1)} %slice.28), channel_id=1, source_target_pairs={{0,28},{4,0},{8,4},{12,8},{16,12},{20,16},{24,20},{28,24},{1,29},{... | collective-permute-start | bytes 294920 | tf_op jit(solution)/shard_map/ppermute | solution.py:35
  57.1 5.7 %collective-permute-start.15 = (bf16[64,1536]{1,0:T(8,128)(2,1)S(1)}, bf16[64,1536]{1,0:T(8,128)(2,1)S(1)}, u32[]{:S(2)}, u32[]{:S(2)}) collective-permute-start(bf16[64,1536]{1,0:T(8,128)(2,1)S(1)} %get-tuple-element.83), channel_id=1, source_target_pairs={{0,32},{32,64},{64,96},{96,0},{1,33},{33,65},{65,97},{97,1},{2,34}... | collective-permute-start | bytes 589832 | tf_op jit(solution)/shard_map/ppermute | solution.py:35
  58.9 8.3 %collective-permute-start.16 = (bf16[64,1536]{1,0:T(8,128)(2,1)S(1)}, bf16[64,1536]{1,0:T(8,128)(2,1)S(1)}, u32[]{:S(2)}, u32[]{:S(2)}) collective-permute-start(bf16[64,1536]{1,0:T(8,128)(2,1)S(1)} %get-tuple-element.84), channel_id=1, source_target_pairs={{0,96},{32,0},{64,32},{96,64},{1,97},{33,1},{65,33},{97,65},{2,98}... | collective-permute-start | bytes 589832 | tf_op jit(solution)/shard_map/ppermute | solution.py:35
  59.2 17.3 %collective-permute-start.19 = (bf16[256,1536]{1,0:T(8,128)(2,1)S(1)}, bf16[256,1536]{1,0:T(8,128)(2,1)S(1)}, u32[]{:S(2)}, u32[]{:S(2)}) collective-permute-start(bf16[256,1536]{1,0:T(8,128)(2,1)S(1)} %get-tuple-element.90), channel_id=1, source_target_pairs={{0,2},{2,0},{1,3},{3,1},{4,6},{6,4},{5,7},{7,5},{8,10},{10,8},{9,1... | collective-permute-start | bytes 2359304 | tf_op jit(solution)/shard_map/ppermute | solution.py:35
  59.9 28.9 %copy-start.4 = (s32[6,12]{1,0:T(8,128)S(1)}, s32[6,12]{1,0:T(8,128)}, u32[]{:S(2)}) copy-start(s32[6,12]{1,0:T(8,128)} %mask.2) | copy-start | bytes 868
  60.0 28.8 %collective-permute-start.25 = (bf16[768,1536]{1,0:T(8,128)(2,1)S(1)}, bf16[768,1536]{1,0:T(8,128)(2,1)S(1)}, u32[]{:S(2)}, u32[]{:S(2)}) collective-permute-start(bf16[768,1536]{1,0:T(8,128)(2,1)S(1)} %get-tuple-element.98.refs_4_.in0), channel_id=1, source_target_pairs={{0,1},{1,0},{2,3},{3,2},{4,5},{5,4},{6,7},{7,6},{8,9},{9,8},{10,11... | collective-permute-start | bytes 7077896 | tf_op jit(solution)/shard_map/ppermute | solution.py:35
  60.1 9.9 %collective-permute-start.18 = (bf16[64,1536]{1,0:T(8,128)(2,1)S(1)}, bf16[64,1536]{1,0:T(8,128)(2,1)S(1)}, u32[]{:S(2)}, u32[]{:S(2)}) collective-permute-start(bf16[64,1536]{1,0:T(8,128)(2,1)S(1)} %get-tuple-element.89), channel_id=1, source_target_pairs={{0,96},{32,0},{64,32},{96,64},{1,97},{33,1},{65,33},{97,65},{2,98}... | collective-permute-start | bytes 589832 | tf_op jit(solution)/shard_map/ppermute | solution.py:35
  67.3 5.7 %collective-permute-start.17 = (bf16[64,1536]{1,0:T(8,128)(2,1)S(1)}, bf16[64,1536]{1,0:T(8,128)(2,1)S(1)}, u32[]{:S(2)}, u32[]{:S(2)}) collective-permute-start(bf16[64,1536]{1,0:T(8,128)(2,1)S(1)} %add_convert_fusion.6), channel_id=1, source_target_pairs={{0,32},{32,64},{64,96},{96,0},{1,33},{33,65},{65,97},{97,1},{2,34}... | collective-permute-start | bytes 589832 | tf_op jit(solution)/shard_map/ppermute | solution.py:35
  67.4 10.8 %collective-permute-start.14 = (bf16[64,1536]{1,0:T(8,128)(2,1)S(1)}, bf16[64,1536]{1,0:T(8,128)(2,1)S(1)}, u32[]{:S(2)}, u32[]{:S(2)}) collective-permute-start(bf16[64,1536]{1,0:T(8,128)(2,1)S(1)} %get-tuple-element.80), channel_id=1, source_target_pairs={{0,32},{32,64},{64,96},{96,0},{1,33},{33,65},{65,97},{97,1},{2,34}... | collective-permute-start | bytes 589832 | tf_op jit(solution)/shard_map/ppermute | solution.py:35
  76.6 7.2 %collective-permute-start.20 = (bf16[64,1536]{1,0:T(8,128)(2,1)S(1)}, bf16[64,1536]{1,0:T(8,128)(2,1)S(1)}, u32[]{:S(2)}, u32[]{:S(2)}) collective-permute-start(bf16[64,1536]{1,0:T(8,128)(2,1)S(1)} %add_convert_fusion.5), channel_id=1, source_target_pairs={{0,96},{32,0},{64,32},{96,64},{1,97},{33,1},{65,33},{97,65},{2,98}... | collective-permute-start | bytes 589832 | tf_op jit(solution)/shard_map/ppermute | solution.py:35
  77.7 7.3 %collective-permute-start.21 = (bf16[64,1536]{1,0:T(8,128)(2,1)S(1)}, bf16[64,1536]{1,0:T(8,128)(2,1)S(1)}, u32[]{:S(2)}, u32[]{:S(2)}) collective-permute-start(bf16[64,1536]{1,0:T(8,128)(2,1)S(1)} %add_convert_fusion.4), channel_id=1, source_target_pairs={{0,128},{128,0},{1,129},{129,1},{2,130},{130,2},{3,131},{131,3},{4... | collective-permute-start | bytes 589832 | tf_op jit(solution)/shard_map/ppermute | solution.py:35
  85.0 8.6 %collective-permute-start.24 = (bf16[64,1536]{1,0:T(8,128)(2,1)S(1)}, bf16[64,1536]{1,0:T(8,128)(2,1)S(1)}, u32[]{:S(2)}, u32[]{:S(2)}) collective-permute-start(bf16[64,1536]{1,0:T(8,128)(2,1)S(1)} %multiply_convert_fusion.refs_0_), channel_id=1, source_target_pairs={{0,96},{32,0},{64,32},{96,64},{1,97},{33,1},{65,33},{97,65},{2,98}... | collective-permute-start | bytes 589832 | tf_op jit(solution)/shard_map/ppermute | solution.py:35
  85.3 8.7 %collective-permute-start.23 = (bf16[64,1536]{1,0:T(8,128)(2,1)S(1)}, bf16[64,1536]{1,0:T(8,128)(2,1)S(1)}, u32[]{:S(2)}, u32[]{:S(2)}) collective-permute-start(bf16[64,1536]{1,0:T(8,128)(2,1)S(1)} %multiply_convert_fusion.refs_0_), channel_id=1, source_target_pairs={{0,32},{32,64},{64,96},{96,0},{1,33},{33,65},{65,97},{97,1},{2,34}... | collective-permute-start | bytes 589832 | tf_op jit(solution)/shard_map/ppermute | solution.py:35
  88.4 7.2 %collective-permute-start.22 = (bf16[64,1536]{1,0:T(8,128)(2,1)S(1)}, bf16[64,1536]{1,0:T(8,128)(2,1)S(1)}, u32[]{:S(2)}, u32[]{:S(2)}) collective-permute-start(bf16[64,1536]{1,0:T(8,128)(2,1)S(1)} %multiply_convert_fusion.refs_0_), channel_id=1, source_target_pairs={{0,128},{128,0},{1,129},{129,1},{2,130},{130,2},{3,131},{131,3},{4... | collective-permute-start | bytes 589832 | tf_op jit(solution)/shard_map/ppermute | solution.py:35
  95.5 7.0 %collective-permute-start.27 = (bf16[64,1536]{1,0:T(8,128)(2,1)S(1)}, bf16[64,1536]{1,0:T(8,128)(2,1)S(1)}, u32[]{:S(2)}, u32[]{:S(2)}) collective-permute-start(bf16[64,1536]{1,0:T(8,128)(2,1)S(1)} %collective-permute-done.22.refs_1_), channel_id=1, source_target_pairs={{0,96},{32,0},{64,32},{96,64},{1,97},{33,1},{65,33},{97,65},{2,98}... | collective-permute-start | bytes 589832 | tf_op jit(solution)/shard_map/ppermute | solution.py:35
  96.3 8.1 %collective-permute-start.26 = (bf16[64,1536]{1,0:T(8,128)(2,1)S(1)}, bf16[64,1536]{1,0:T(8,128)(2,1)S(1)}, u32[]{:S(2)}, u32[]{:S(2)}) collective-permute-start(bf16[64,1536]{1,0:T(8,128)(2,1)S(1)} %collective-permute-done.22.refs_1_), channel_id=1, source_target_pairs={{0,32},{32,64},{64,96},{96,0},{1,33},{33,65},{65,97},{97,1},{2,34}... | collective-permute-start | bytes 589832 | tf_op jit(solution)/shard_map/ppermute | solution.py:35
  98.8 5.7 %collective-permute-start.28 = (bf16[64,1536]{1,0:T(8,128)(2,1)S(1)}, bf16[64,1536]{1,0:T(8,128)(2,1)S(1)}, u32[]{:S(2)}, u32[]{:S(2)}) collective-permute-start(bf16[64,1536]{1,0:T(8,128)(2,1)S(1)} %collective-permute-done.23.refs_2_), channel_id=1, source_target_pairs={{0,32},{32,64},{64,96},{96,0},{1,33},{33,65},{65,97},{97,1},{2,34}... | collective-permute-start | bytes 589832 | tf_op jit(solution)/shard_map/ppermute | solution.py:35
  102.5 6.9 %collective-permute-start.29 = (bf16[64,1536]{1,0:T(8,128)(2,1)S(1)}, bf16[64,1536]{1,0:T(8,128)(2,1)S(1)}, u32[]{:S(2)}, u32[]{:S(2)}) collective-permute-start(bf16[64,1536]{1,0:T(8,128)(2,1)S(1)} %collective-permute-done.27.refs_5_), channel_id=1, source_target_pairs={{0,96},{32,0},{64,32},{96,64},{1,97},{33,1},{65,33},{97,65},{2,98}... | collective-permute-start | bytes 589832 | tf_op jit(solution)/shard_map/ppermute | solution.py:35
  112.9 12.1 %collective-permute-start.34 = (bf16[512,1536]{1,0:T(8,128)(2,1)S(1)}, bf16[512,1536]{1,0:T(8,128)(2,1)S(1)}, u32[]{:S(2)}, u32[]{:S(2)}) collective-permute-start(bf16[512,1536]{1,0:T(8,128)(2,1)S(1)} %get-tuple-element.110.in1), channel_id=1, source_target_pairs={{0,1},{1,0},{2,3},{3,2},{4,5},{5,4},{6,7},{7,6},{8,9},{9,8},{10,11... | collective-permute-start | bytes 4718600 | tf_op jit(solution)/shard_map/ppermute | solution.py:35
  113.0 8.5 %collective-permute-start.30 = (bf16[64,1536]{1,0:T(8,128)(2,1)S(1)}, bf16[64,1536]{1,0:T(8,128)(2,1)S(1)}, u32[]{:S(2)}, u32[]{:S(2)}) collective-permute-start(bf16[64,1536]{1,0:T(8,128)(2,1)S(1)} %get-tuple-element.107), channel_id=1, source_target_pairs={{0,4},{4,8},{8,12},{12,16},{16,20},{20,24},{24,28},{28,0},{1,5},{5... | collective-permute-start | bytes 589832 | tf_op jit(solution)/shard_map/ppermute | solution.py:35
  113.1 8.6 %collective-permute-start.32 = (bf16[64,1536]{1,0:T(8,128)(2,1)S(1)}, bf16[64,1536]{1,0:T(8,128)(2,1)S(1)}, u32[]{:S(2)}, u32[]{:S(2)}) collective-permute-start(bf16[64,1536]{1,0:T(8,128)(2,1)S(1)} %get-tuple-element.109), channel_id=1, source_target_pairs={{0,28},{4,0},{8,4},{12,8},{16,12},{20,16},{24,20},{28,24},{1,29},{... | collective-permute-start | bytes 589832 | tf_op jit(solution)/shard_map/ppermute | solution.py:35
  121.6 8.2 %collective-permute-start.31 = (bf16[64,1536]{1,0:T(8,128)(2,1)S(1)}, bf16[64,1536]{1,0:T(8,128)(2,1)S(1)}, u32[]{:S(2)}, u32[]{:S(2)}) collective-permute-start(bf16[64,1536]{1,0:T(8,128)(2,1)S(1)} %add_convert_fusion.3), channel_id=1, source_target_pairs={{0,4},{4,8},{8,12},{12,16},{16,20},{20,24},{24,28},{28,0},{1,5},{5... | collective-permute-start | bytes 589832 | tf_op jit(solution)/shard_map/ppermute | solution.py:35
  121.7 8.1 %collective-permute-start.33 = (bf16[64,1536]{1,0:T(8,128)(2,1)S(1)}, bf16[64,1536]{1,0:T(8,128)(2,1)S(1)}, u32[]{:S(2)}, u32[]{:S(2)}) collective-permute-start(bf16[64,1536]{1,0:T(8,128)(2,1)S(1)} %add_convert_fusion.2), channel_id=1, source_target_pairs={{0,28},{4,0},{8,4},{12,8},{16,12},{20,16},{24,20},{28,24},{1,29},{... | collective-permute-start | bytes 589832 | tf_op jit(solution)/shard_map/ppermute | solution.py:35
  129.8 6.0 %collective-permute-start.35 = (bf16[64,1536]{1,0:T(8,128)(2,1)S(1)}, bf16[64,1536]{1,0:T(8,128)(2,1)S(1)}, u32[]{:S(2)}, u32[]{:S(2)}) collective-permute-start(bf16[64,1536]{1,0:T(8,128)(2,1)S(1)} %add_convert_fusion.1), channel_id=1, source_target_pairs={{0,28},{4,0},{8,4},{12,8},{16,12},{20,16},{24,20},{28,24},{1,29},{... | collective-permute-start | bytes 589832 | tf_op jit(solution)/shard_map/ppermute | solution.py:35
  132.5 7.0 %collective-permute-start.36 = (bf16[64,1536]{1,0:T(8,128)(2,1)S(1)}, bf16[64,1536]{1,0:T(8,128)(2,1)S(1)}, u32[]{:S(2)}, u32[]{:S(2)}) collective-permute-start(bf16[64,1536]{1,0:T(8,128)(2,1)S(1)} %add_convert_fusion), channel_id=1, source_target_pairs={{0,4},{4,8},{8,12},{12,16},{16,20},{20,24},{24,28},{28,0},{1,5},{5... | collective-permute-start | bytes 589832 | tf_op jit(solution)/shard_map/ppermute | solution.py:35
  135.8 5.9 %collective-permute-start.38 = (bf16[32,1536]{1,0:T(8,128)(2,1)S(1)}, bf16[32,1536]{1,0:T(8,128)(2,1)S(1)}, u32[]{:S(2)}, u32[]{:S(2)}) collective-permute-start(bf16[32,1536]{1,0:T(8,128)(2,1)S(1)} %add_convert_fusion.9), channel_id=1, source_target_pairs={{0,28},{4,0},{8,4},{12,8},{16,12},{20,16},{24,20},{28,24},{1,29},{... | collective-permute-start | bytes 294920 | tf_op jit(solution)/shard_map/ppermute | solution.py:35
  141.8 6.3 %collective-permute-start.37 = (bf16[32,1536]{1,0:T(8,128)(2,1)S(1)}, bf16[32,1536]{1,0:T(8,128)(2,1)S(1)}, u32[]{:S(2)}, u32[]{:S(2)}) collective-permute-start(bf16[32,1536]{1,0:T(8,128)(2,1)S(1)} %get-tuple-element.119), channel_id=1, source_target_pairs={{0,4},{4,8},{8,12},{12,16},{16,20},{20,24},{24,28},{28,0},{1,5},{5... | collective-permute-start | bytes 294920 | tf_op jit(solution)/shard_map/ppermute | solution.py:35
  141.8 6.2 %collective-permute-start.39 = (bf16[32,1536]{1,0:T(8,128)(2,1)S(1)}, bf16[32,1536]{1,0:T(8,128)(2,1)S(1)}, u32[]{:S(2)}, u32[]{:S(2)}) collective-permute-start(bf16[32,1536]{1,0:T(8,128)(2,1)S(1)} %get-tuple-element.120), channel_id=1, source_target_pairs={{0,2},{2,0},{1,3},{3,1},{4,6},{6,4},{5,7},{7,5},{8,10},{10,8},{9,1... | collective-permute-start | bytes 294920 | tf_op jit(solution)/shard_map/ppermute | solution.py:35
